TPU v7x, 128 devices: a whole 4x4x4 slice. The times are simulated.
128 devices in a mesh: row: 4 (over x), rad: 32 (over y, z, core).
Axes of the slice: x: 4, y: 4, z: 4, core: 2. Of those that a mesh axis runs over, the one named last changes fastest.
Arguments:
- adjoint_cells: float32 [4, 256, 17, 5, 512], P('row', 'rad'), may hold values from -6 to 6
- flux_jacobian: bfloat16 [4, 256, 17, 5, 5, 512], P('row', 'rad'), may hold values from -2 to 2
- dissipation: float32 [4, 256, 512], P('row', 'rad'), may hold values from 0.2 to 2
- face_rows: float32 [2048, 17, 5, 128], P(('row', 'rad')), may hold values from -6 to 6
- owners: int32 [2048, 17, 3], P(('row', 'rad')), may hold values from 0 to 511, all different within a row; in each aligned block of 272 rows (0 to 271, 272 to 543, ..., all dimensions but the last counted through in order) at most 2 rows name the same one
- margin_weights: float32 [2048, 17, 3], P(('row', 'rad')), may hold values from 0.25 to 1
- transposed_maps: bfloat16 [512, 128, 128], P(('row', 'rad')), may hold values from -0.5 to 0.5
Outputs:
- cell_gradient: float32 [4, 256, 17, 5, 512], P('row', 'rad')
- face_gradient: float32 [2048, 17, 5, 128], P(('row', 'rad'))
Inputs may be any that keep to these rules, and one draw needn't show every extreme that they name: `owners`: each row names 3 different stator blocks; among the rows of one device's face tiles no block is named more than 2 times, and some block exactly 2 times.
All inputs are finite; a program needn't handle non-finite values.
Results may differ from a plain program's by a relative error of at most 0.002.
Values may be sent and summed in bfloat16 or wider, within the bound.
No kernel may reach another device: no remote copies, remote signals or barrier semaphores. Data moves between devices by JAX's collectives and lax.ppermute only.
A program may use at most 64 MiB of HBM per device.

v0:
```python
import math

import jax
import jax.numpy as jnp
from jax import lax
from jax.sharding import PartitionSpec as P

NT = 17
NH = 5
F = 5
FACE = 128
K = 3


def padded_2(value, sides, width):
    for axis, dim in sides:
        size, length = (lax.axis_size(axis), value.shape[dim])
        up = [(i, (i + 1) % size) for i in range(size - 1)]
        down = [(j, i) for i, j in up]
        last = lax.slice_in_dim(value, length - width, length, axis=dim)
        initial = lax.slice_in_dim(value, 0, width, axis=dim)
        before = lax.ppermute(last, axis, up)
        after = lax.ppermute(initial, axis, down)
        value = jnp.concatenate([before, value, after], axis=dim)
    return value


def derivative_matrix():
    instance = jnp.arange(NT)
    offset = (instance[:, None] - instance[None, :]).astype(jnp.float32)
    harmonic = jnp.arange(1, NH + 1).astype(jnp.float32)
    angles = 2.0 * math.pi * harmonic * offset[..., None] / NT
    return -(2.0 * 0.5 / NT) * jnp.sum(harmonic * jnp.sin(angles), axis=-1)


def time_adjoint(field):
    derivative = derivative_matrix()
    flat = field.reshape((-1,) + field.shape[-3:])
    result = jnp.einsum("st,asfn->atfn", derivative, flat, precision=lax.Precision.HIGHEST)
    return result.reshape(field.shape)


def body(
    adjoint_cells, flux_jacobian, dissipation, face_rows, owners, margin_weights, transposed_maps
):
    sources = lax.axis_size(("row", "rad"))
    own_blocks = transposed_maps.shape[0]
    own_tiles = face_rows.shape[0]
    all_blocks = sources * own_blocks
    entries = own_tiles * NT * K
    capacity = max(2, (5 * entries + 4 * all_blocks - 1) // (4 * all_blocks))
    width = F * FACE
    target = owners.reshape(entries)
    block_hits = (target[:, None] == jnp.arange(all_blocks, dtype=jnp.int32)[None, :]).astype(
        jnp.int32
    )
    slot_rank = jnp.sum((jnp.cumsum(block_hits, axis=0) - block_hits) * block_hits, axis=1)
    position = target * capacity + slot_rank
    sent_rows = jnp.repeat(face_rows.astype(jnp.bfloat16).reshape(own_tiles * NT, width), K, axis=0)
    outgoing = jnp.zeros((all_blocks * capacity, width), jnp.bfloat16).at[position].set(sent_rows)
    arrived = lax.all_to_all(
        outgoing.reshape(sources, own_blocks * capacity, width),
        ("row", "rad"),
        split_axis=0,
        concat_axis=0,
        tiled=True,
    )
    blocks_view = arrived.reshape(sources, own_blocks, capacity, F, FACE)
    products = jnp.einsum(
        "dbcfi,bij->dbcfj", blocks_view, transposed_maps, preferred_element_type=jnp.float32
    )
    products = products.reshape(sources, own_blocks * capacity, width)
    returned = lax.all_to_all(products, ("row", "rad"), split_axis=0, concat_axis=0, tiled=True)
    time_cells = time_adjoint(adjoint_cells)
    jac_term = jnp.sum(flux_jacobian.astype(jnp.float32) * adjoint_cells[..., :, None, :], axis=-3)
    weighted_field = dissipation[:, :, None, None, :] * adjoint_cells
    padded = padded_2(weighted_field, (("rad", 1),), 1)
    laplace = padded[:, 2:] - 2.0 * weighted_field + padded[:, :-2]
    cell_gradient = time_cells + jac_term - laplace
    time_faces = time_adjoint(face_rows)
    values = returned.reshape(all_blocks * capacity, width)[position]
    scaled = values * margin_weights.reshape(entries)[:, None]
    interface = jnp.sum(scaled.reshape(own_tiles, NT, K, F, FACE), axis=2)
    face_gradient = time_faces + interface
    return (cell_gradient, face_gradient)


def solution(mesh):
    placed = (
        P("row", "rad", None, None, None),
        P("row", "rad", None, None, None, None),
        P("row", "rad", None),
        P(("row", "rad"), None, None, None),
        P(("row", "rad"), None, None),
        P(("row", "rad"), None, None),
        P(("row", "rad"), None, None),
    )
    return jax.shard_map(
        body,
        mesh=mesh,
        in_specs=placed,
        out_specs=(P("row", "rad", None, None, None), P(("row", "rad"), None, None, None)),
        check_vma=False,
    )
```

profile of v0, /device:TPU:22, one launch (start us, length us, event | category | flops | bytes accessed | tf_op | source)
XLA Modules:
  0.0 109.0 jit_solution(4846291264703268551)
XLA Ops:
  0.6 1.0 copy.70
  1.6 0.7 broadcast_multiply_fusion
  2.6 0.3 iota_compare_fusion
  3.1 1.3 %fusion = s32[512,7,128]{0,1,2:T(8,128)S(1)} fusion(s32[512,7,128]{0,2,1:T(8,128)S(1)} %bitcast.46), kind=kOutput, calls=%fused_computation.4 | output fusion | flops 58261504 | bytes 3670016 | tf_op jit(solution)/shard_map/reduce-window
  4.5 0.2 broadcast_add_fusion
  4.7 1.1 copy.72
  5.8 0.6 fusion.8
  7.1 0.4 broadcast_in_dim.5
  7.5 0.9 reshape.128
  8.4 5.9 %scatter_custom_fusion = bf16[1024,640]{1,0:T(8,128)(2,1)S(1)} fusion(s32[816]{0:T(1024)S(1)} %fusion.23, bf16[816,640]{1,0:T(8,128)(2,1)S(1)} %reshape.128, bf16[]{:T(256)} %constant.10.clone.1), kind=kCustom, calls=%fused_computation.25 | custom fusion | bytes 1310722 | tf_op jit(solution)/shard_map/scatter | solution.py:60
  14.4 28.5 %all_to_all.10 = bf16[128,8,640]{2,1,0:T(8,128)(2,1)S(1)} all-to-all(bf16[128,8,640]{2,1,0:T(8,128)(2,1)S(1)} %bitcast.48), channel_id=1, replica_groups=mesh['row'=4,'rad'=32] {'row','rad'}, dimensions={0} | all-to-all | bytes 2621440 | tf_op jit(solution)/shard_map/all_to_all | solution.py:61
  42.9 1.8 %copy.74 = bf16[128,8,640]{0,2,1:T(8,128)(2,1)} copy(bf16[128,8,640]{2,1,0:T(8,128)(2,1)S(1)} %all_to_all.10) | data formatting | bytes 2621440 | tf_op jit(solution)/shard_map/all_to_all | solution.py:61
  44.7 1.9 %fusion.15 = f32[4,128,2,5,128]{1,4,3,2,0:T(8,128)S(1)} fusion(bf16[128,4,2,5,128]{0,4,3,2,1:T(8,128)(2,1)} %bitcast.49, bf16[4,128,128]{2,1,0:T(8,128)(2,1)S(1)} %copy-done), kind=kOutput, calls=%fused_computation.28 | convolution fusion | flops 167772160 | bytes 4063232 | tf_op jit(solution)/shard_map/dbcfi,bij->dbcfj/dot_general | solution.py:69
  46.6 2.3 %copy.77 = f32[128,8,640]{2,1,0:T(8,128)} copy(f32[128,8,640]{0,2,1:T(8,128)S(1)} %bitcast.45) | data formatting | bytes 5242880 | tf_op jit(solution)/shard_map/reshape | solution.py:72
  48.9 8.6 %all-to-all-start.1 = ((f32[128,8,640]{2,1,0:T(8,128)}), f32[128,8,640]{2,1,0:T(8,128)S(1)}, u32[]{:S(2)}, u32[]{:S(2)}) async-start(f32[128,8,640]{2,1,0:T(8,128)} %copy.77), calls=%async_computation.1 | async-start | bytes 5242880 | tf_op jit(solution)/shard_map/all_to_all | solution.py:73
  57.5 2.2 %copy_multiply_fusion = f32[1,8,17,5,512]{4,2,3,1,0:T(8,128)S(1)} fusion(f32[1,8,17,5,512]{4,1,3,2,0:T(8,128)} %param.7, f32[8,512]{1,0:T(8,128)S(1)} %bitcast.53), kind=kLoop, calls=%fused_computation.12 | loop fusion | flops 348160 | bytes 2801664 | tf_op jit(solution)/shard_map/mul | solution.py:76
  59.7 1.2 %copy-done.2 = f32[1,8,17,5,512]{4,2,3,1,0:T(8,128)} copy-done((f32[1,8,17,5,512]{4,2,3,1,0:T(8,128)}, f32[1,8,17,5,512]{4,2,3,1,0:T(8,128)S(1)}, u32[]{:S(2)}) %copy-start.2) | copy-done | bytes 1392664
  61.0 0.7 fusion.26
  61.7 5.1 %collective-permute-start = (f32[1,1,17,5,512]{4,2,3,1,0:T(8,128)}, f32[1,1,17,5,512]{4,2,3,1,0:T(8,128)S(1)}, u32[]{:S(2)}, u32[]{:S(2)}) collective-permute-start(f32[1,1,17,5,512]{4,2,3,1,0:T(8,128)} %get-tuple-element.12), channel_id=1, source_target_pairs={{1,0},{2,1},{3,2},{4,3},{5,4},{6,5},{7,6},{8,7},{9,8},{10,9},{11,1... | collective-permute-start | bytes 522248 | tf_op jit(solution)/shard_map/ppermute | solution.py:23
  66.8 2.1 %collective-permute-start.1 = (f32[1,1,17,5,512]{4,2,3,1,0:T(8,128)S(1)}, f32[1,1,17,5,512]{4,2,3,1,0:T(8,128)S(1)}, u32[]{:S(2)}, u32[]{:S(2)}) collective-permute-start(f32[1,1,17,5,512]{4,2,3,1,0:T(8,128)S(1)} %get-tuple-element.13), channel_id=1, source_target_pairs={{0,1},{1,2},{2,3},{3,4},{4,5},{5,6},{6,7},{7,8},{8,9},{9,10},{10,1... | collective-permute-start | bytes 522248 | tf_op jit(solution)/shard_map/ppermute | solution.py:22
  68.9 0.9 copy.78
  69.8 3.7 %multiply_reduce_fusion = f32[8,17,5,512]{3,0,2,1:T(8,128)S(1)} fusion(bf16[1,8,17,5,5,512]{5,1,4,3,2,0:T(8,128)(2,1)} %param.8, f32[8,17,5,512]{3,0,2,1:T(8,128)} %bitcast.43), kind=kLoop, calls=%fused_computation.2 | loop fusion | flops 4874240 | bytes 6266880 | tf_op jit(solution)/shard_map/reduce_sum | solution.py:75
  73.5 0.3 multiply_reduce_fusion.2
  73.8 15.4 %collective-permute-done = f32[1,1,17,5,512]{4,2,3,1,0:T(8,128)S(1)} collective-permute-done((f32[1,1,17,5,512]{4,2,3,1,0:T(8,128)}, f32[1,1,17,5,512]{4,2,3,1,0:T(8,128)S(1)}, u32[]{:S(2)}, u32[]{:S(2)}) %collective-permute-start) | collective-permute-done | bytes 174112 | tf_op jit(solution)/shard_map/ppermute | solution.py:23
  89.2 4.1 %collective-permute-done.1 = f32[1,1,17,5,512]{4,2,3,1,0:T(8,128)S(1)} collective-permute-done((f32[1,1,17,5,512]{4,2,3,1,0:T(8,128)S(1)}, f32[1,1,17,5,512]{4,2,3,1,0:T(8,128)S(1)}, u32[]{:S(2)}, u32[]{:S(2)}) %collective-permute-start.1) | collective-permute-done | bytes 174112 | tf_op jit(solution)/shard_map/ppermute | solution.py:22
  93.3 3.4 %fusion.3 = f32[1,8,17,5,512]{4,2,3,1,0:T(8,128)S(1)} fusion(f32[1,8,17,5,512]{4,2,3,1,0:T(8,128)S(1)} %copy-done.3, f32[1,1,17,5,512]{4,2,3,1,0:T(8,128)S(1)} %collective-permute-done.1, f32[1,1,17,5,512]{4,2,3,1,0:T(8,128)S(1)} %collective-permute-done, f32[8,17,5,512]{3,0,2,1:T(8,128)S(1)} %multiply_reduce_fusion, f32[8,17,5,512]{3,0,2,1:T(8,128)S(1)} %bitcast.44, ...), kind=kOutput, calls=%fused_computation.8 | convolution fusion | flops 73462048 | bytes 5919876 | tf_op jit(solution)/shard_map/st,asfn->atfn/dot_general | solution.py:39
  96.7 1.9 %copy.80 = f32[1,8,17,5,512]{4,1,3,2,0:T(8,128)} copy(f32[1,8,17,5,512]{4,2,3,1,0:T(8,128)S(1)} %fusion.3) | data formatting | bytes 2785280
  98.5 3.8 %gather_fusion = f32[816,640]{1,0:T(8,128)} fusion(f32[1024,640]{1,0:T(8,128)S(1)} %bitcast.42, s32[1024]{0:T(1024)S(1)} %pad_clamp_fusion), kind=kCustom, calls=%fused_computation | custom fusion | bytes 4181184 | tf_op jit(solution)/shard_map/gather | solution.py:81
  102.4 2.4 %gather.6 = f32[16,17,3,5,128]{4,3,2,1,0:T(8,128)S(1)} reshape(f32[816,640]{1,0:T(8,128)} %gather_fusion) | data formatting | bytes 4177920 | tf_op jit(solution)/shard_map/gather | solution.py:81
  104.8 2.1 %multiply_reduce_fusion.1 = f32[16,17,5,128]{3,2,1,0:T(8,128)S(1)} fusion(f32[16,17,3,5,128]{4,3,2,1,0:T(8,128)S(1)} %gather.6, f32[16,17,3]{2,1,0:T(8,128)} %copy.78), kind=kLoop, calls=%fused_computation.3 | loop fusion | flops 870400 | bytes 2788544 | tf_op jit(solution)/shard_map/reduce_sum | solution.py:83
  106.9 1.2 %fusion.11 = f32[16,17,5,128]{3,1,2,0:T(8,128)S(1)} fusion(f32[16,17,5,128]{3,2,1,0:T(8,128)S(1)} %multiply_reduce_fusion.1, f32[16,17,5,128]{3,0,2,1:T(8,128)S(1)} %copy-done.5, f32[17,17]{1,0:T(8,128)S(1)} %multiply_reduce_fusion.2), kind=kOutput, calls=%fused_computation.22 | convolution fusion | flops 35686688 | bytes 2090116 | tf_op jit(solution)/shard_map/st,asfn->atfn/dot_general | solution.py:39
  108.1 1.0 copy.81
  (30 shorter events, 1.3 us)
Async XLA Ops:
  0.6 44.1 %copy-start = (bf16[4,128,128]{2,1,0:T(8,128)(2,1)S(1)}, bf16[4,128,128]{2,1,0:T(8,128)(2,1)}, u32[]{:S(2)}) copy-start(bf16[4,128,128]{2,1,0:T(8,128)(2,1)} %param.13) | copy-start | bytes 393220
  5.8 1.1 %copy-start.4 = (f32[16,17,5,128]{3,0,2,1:T(8,128)S(1)}, f32[16,17,5,128]{3,0,2,1:T(8,128)}, u32[]{:S(2)}) copy-start(f32[16,17,5,128]{3,0,2,1:T(8,128)} %param.10) | copy-start | bytes 2088964
  48.9 8.6 %copy-start.7 = (f32[1,8,512]{2,1,0:T(8,128)S(1)}, f32[1,8,512]{2,1,0:T(8,128)}, u32[]{:S(2)}) copy-start(f32[1,8,512]{2,1,0:T(8,128)} %param.9) | copy-start | bytes 49156
  48.9 49.6 %all-to-all-start.1 = ((f32[128,8,640]{2,1,0:T(8,128)}), f32[128,8,640]{2,1,0:T(8,128)S(1)}, u32[]{:S(2)}, u32[]{:S(2)}) async-start(f32[128,8,640]{2,1,0:T(8,128)} %copy.77), calls=%async_computation.1 | async-start | bytes 5242880 | tf_op jit(solution)/shard_map/all_to_all | solution.py:73
  57.5 11.4 %copy-start.6 = (f32[16,17,3]{1,0,2:T(8,128)S(1)}, f32[16,17,3]{1,0,2:T(8,128)}, u32[]{:S(2)}) copy-start(f32[16,17,3]{1,0,2:T(8,128)} %param.12) | copy-start | bytes 9796
  59.7 1.3 %copy-start.2 = (f32[1,8,17,5,512]{4,2,3,1,0:T(8,128)}, f32[1,8,17,5,512]{4,2,3,1,0:T(8,128)S(1)}, u32[]{:S(2)}) copy-start(f32[1,8,17,5,512]{4,2,3,1,0:T(8,128)S(1)} %copy_multiply_fusion) | copy-start | bytes 4177924
  61.7 27.5 %collective-permute-start = (f32[1,1,17,5,512]{4,2,3,1,0:T(8,128)}, f32[1,1,17,5,512]{4,2,3,1,0:T(8,128)S(1)}, u32[]{:S(2)}, u32[]{:S(2)}) collective-permute-start(f32[1,1,17,5,512]{4,2,3,1,0:T(8,128)} %get-tuple-element.12), channel_id=1, source_target_pairs={{1,0},{2,1},{3,2},{4,3},{5,4},{6,5},{7,6},{8,7},{9,8},{10,9},{11,1... | collective-permute-start | bytes 522248 | tf_op jit(solution)/shard_map/ppermute | solution.py:23
  66.8 26.5 %collective-permute-start.1 = (f32[1,1,17,5,512]{4,2,3,1,0:T(8,128)S(1)}, f32[1,1,17,5,512]{4,2,3,1,0:T(8,128)S(1)}, u32[]{:S(2)}, u32[]{:S(2)}) collective-permute-start(f32[1,1,17,5,512]{4,2,3,1,0:T(8,128)S(1)} %get-tuple-element.13), channel_id=1, source_target_pairs={{0,1},{1,2},{2,3},{3,4},{4,5},{5,6},{6,7},{7,8},{8,9},{9,10},{10,1... | collective-permute-start | bytes 522248 | tf_op jit(solution)/shard_map/ppermute | solution.py:22
  69.8 23.5 %copy-start.1 = (f32[1,8,17,5,512]{4,1,3,2,0:T(8,128)S(1)}, f32[1,8,17,5,512]{4,1,3,2,0:T(8,128)}, u32[]{:S(2)}) copy-start(f32[1,8,17,5,512]{4,1,3,2,0:T(8,128)} %param.7) | copy-start | bytes 4177924
  69.8 23.5 %copy-start.3 = (f32[1,8,17,5,512]{4,2,3,1,0:T(8,128)S(1)}, f32[1,8,17,5,512]{4,2,3,1,0:T(8,128)}, u32[]{:S(2)}) copy-start(f32[1,8,17,5,512]{4,2,3,1,0:T(8,128)} %copy-done.2) | copy-start | bytes 4177924
  104.8 2.1 %copy-start.5 = (f32[16,17,5,128]{3,0,2,1:T(8,128)S(1)}, f32[16,17,5,128]{3,0,2,1:T(8,128)}, u32[]{:S(2)}) copy-start(f32[16,17,5,128]{3,0,2,1:T(8,128)} %param.10) | copy-start | bytes 2088964
where the time goes:
time: 110 us; the launch traced here: 109 us
  blocking collectives  28.5 us (26%)
  local copies, waits for them, and re-layouts  26.3 us (24%)
  waiting for transfers between devices  19.5 us (18%)
  starting transfers between devices  15.7 us (14%)
  other arithmetic  11.8 us (11%)
  matrix products  6.4 us (6%)
    all_to_all x1, blocking collectives, body(): lax.all_to_all(outgoing.reshape(sources, own_blocks * capacity, width), (...  28.5 us
    ppermute x1, waiting for transfers between devices, padded_2(): after = lax.ppermute(initial, axis, down)  15.4 us
    all_to_all x1, starting transfers between devices, body(): lax.all_to_all(products, ('row', 'rad'), split_axis=0, concat_axis=0, til...  8.55 us
    gather x2, local copies, waits for them, and re-layouts, body(): values = returned.reshape(all_blocks * capacity, width)[position]  6.21 us
    unnamed x21, local copies, waits for them, and re-layouts  6.14 us
    scatter x1, local copies, waits for them, and re-layouts, body(): jnp.zeros((all_blocks * capacity, width), jnp.bfloat16).at[position]  5.95 us
    ppermute x1, starting transfers between devices, padded_2(): after = lax.ppermute(initial, axis, down)  5.06 us
    dot_general x2, matrix products, time_adjoint(): jnp.einsum('st,asfn->atfn', derivative, flat, precision=lax.Precision.HIG...  4.55 us
  transfers between devices with their start and end apart: 3, of which 2 were waited for; matrix products, arithmetic and copies ran while one was open for 12% of the time, Pallas kernels for 0%

commit v1 on v0

v1 whole, which is shorter than its diff:
```python
import math

import jax
import jax.numpy as jnp
import numpy as np
from jax import lax
from jax.experimental import pallas as pl
from jax.experimental.pallas import tpu as pltpu
from jax.sharding import Mesh
from jax.sharding import PartitionSpec as P

NT = 17
NH = 5
F = 5
FACE = 128
K = 3
TILES = 16
LAYERS = 8
NP = 512
BLOCKS = 512
CAP = 2
ROWS = TILES * NT
WIDTH = F * FACE
SLOTS = BLOCKS * CAP
PEERS = 16
GROUP = BLOCKS // PEERS

SPREAD = ("x", "y")
SHARED = ("z", "core")
RADIAL = ("y", "z", "core")
f32 = jnp.float32
bf16 = jnp.bfloat16


def offset_weights():
    m = np.arange(1, NT // 2 + 1, dtype=np.float64)[:, None]
    h = np.arange(1, NH + 1, dtype=np.float64)[None, :]
    return [float(v) for v in -(2.0 * 0.5 / NT) * np.sum(h * np.sin(2.0 * math.pi * h * m / NT), axis=1)]


def time_sum(values):
    weights = offset_weights()
    out = []
    for t in range(NT):
        total = None
        for m, w in enumerate(weights, start=1):
            term = (values[(t + m) % NT] - values[(t - m) % NT]) * w
            total = term if total is None else total + term
        out.append(total)
    return out


def lane_rows(ref):
    table = ref[...].astype(f32).reshape(K * TILES, NT)
    lane = lax.broadcasted_iota(jnp.int32, (NT, ROWS), 1)
    pick = (lane // TILES == lax.broadcasted_iota(jnp.int32, (NT, ROWS), 0)).astype(f32)
    spread = jnp.dot(table, pick, precision=lax.Precision.HIGHEST, preferred_element_type=f32)
    spread = spread.reshape(K, TILES, ROWS)
    sub = lax.broadcasted_iota(jnp.int32, (K, TILES, ROWS), 1)
    col = lax.broadcasted_iota(jnp.int32, (K, TILES, ROWS), 2)
    return jnp.sum(jnp.where(col % TILES == sub, spread, 0.0), axis=1)


def dispatch_kernel(face_ref, owner_ref, out_ref):
    owner = lane_rows(owner_ref).astype(jnp.int32)
    block = lax.broadcasted_iota(jnp.int32, (BLOCKS, ROWS), 0)
    hit = (owner[0:1] == block) | (owner[1:2] == block) | (owner[2:3] == block)
    hit = jnp.where(hit, 1.0, 0.0)
    earlier = lax.broadcasted_iota(jnp.int32, (ROWS, ROWS), 0) < lax.broadcasted_iota(
        jnp.int32, (ROWS, ROWS), 1
    )
    earlier = jnp.where(earlier, 1.0, 0.0).astype(bf16)
    rank = jnp.dot(hit.astype(bf16), earlier, preferred_element_type=f32)
    first = jnp.where(rank < 0.5, hit, 0.0).reshape(BLOCKS // 8, 8, ROWS)
    second = jnp.where(rank > 0.5, hit, 0.0).reshape(BLOCKS // 8, 8, ROWS)
    select = jnp.stack([first, second], axis=1).reshape(SLOTS, ROWS).astype(bf16)
    rows = [face_ref[:, f].reshape(ROWS, FACE).astype(bf16) for f in range(F)]
    rows = jnp.concatenate(rows, axis=1)
    out_ref[...] = jnp.dot(select, rows, preferred_element_type=f32).astype(bf16)


def weights_kernel(face_ref, owner_ref, margin_ref, high_ref, low_ref, time_ref):
    both = jnp.concatenate([lane_rows(owner_ref), lane_rows(margin_ref), jnp.zeros((2, ROWS), f32)], axis=0)
    both = both.T
    slot = lax.broadcasted_iota(jnp.int32, (ROWS, SLOTS), 1)
    block = (slot // 16 * 8 + slot % 8).astype(f32)
    hit = jnp.zeros((ROWS, SLOTS), f32)
    weight = jnp.zeros((ROWS, SLOTS), f32)
    for k in range(K):
        same = both[:, k : k + 1] == block
        hit = jnp.where(same, 1.0, hit)
        weight = jnp.where(same, both[:, K + k : K + k + 1], weight)
    earlier = lax.broadcasted_iota(jnp.int32, (ROWS, ROWS), 1) < lax.broadcasted_iota(
        jnp.int32, (ROWS, ROWS), 0
    )
    earlier = jnp.where(earlier, 1.0, 0.0).astype(bf16)
    rank = jnp.dot(earlier, hit.astype(bf16), preferred_element_type=f32)
    own = (slot // 8 % 2).astype(f32)
    weight = jnp.where(jnp.abs(rank - own) < 0.5, weight, 0.0)
    high = weight.astype(bf16)
    high_ref[...] = high
    low_ref[...] = (weight - high.astype(f32)).astype(bf16)
    for f in range(F):
        total = time_sum([face_ref[t, f] for t in range(NT)])
        for t in range(NT):
            time_ref[t, f] = total[t]


def maps_kernel(rows_ref, maps_ref, out_ref):
    sub = lax.broadcasted_iota(jnp.int32, (PEERS, 16, FACE), 1) % 8
    for g in range(GROUP // 8):
        maps = maps_ref[8 * g : 8 * g + 8].reshape(8 * FACE, FACE)
        for f in range(F):
            lanes = slice(f * FACE, (f + 1) * FACE)
            rows = rows_ref[:, 16 * g : 16 * g + 16, lanes].astype(f32)
            parts = [jnp.where(sub == q, rows, 0.0).reshape(PEERS * 16, FACE).astype(bf16) for q in range(8)]
            result = jnp.dot(jnp.concatenate(parts, axis=1), maps, preferred_element_type=f32)
            out_ref[:, 16 * g : 16 * g + 16, lanes] = result.astype(bf16).reshape(PEERS, 16, FACE)


def combine_kernel(rows_ref, high_ref, low_ref, time_ref, out_ref):
    rows = rows_ref[...]
    total = jnp.dot(high_ref[...], rows, preferred_element_type=f32)
    total = total + jnp.dot(low_ref[...], rows, preferred_element_type=f32)
    for f in range(F):
        out_ref[:, f] = time_ref[:, f] + total[:, f * FACE : (f + 1) * FACE].reshape(NT, TILES, FACE)


def edges_kernel(cells_ref, dissipation_ref, first_ref, last_ref):
    count = NT * F
    first_ref[...] = cells_ref[pl.ds(0, count, stride=LAYERS), :] * dissipation_ref[0:1, :]
    last_ref[...] = cells_ref[pl.ds(LAYERS - 1, count, stride=LAYERS), :] * dissipation_ref[LAYERS - 1 :, :]


def cells_kernel(cells_ref, jac_ref, dissipation_ref, before_ref, after_ref, out_ref):
    dissipation = dissipation_ref[...]
    layer = lax.broadcasted_iota(jnp.int32, dissipation.shape, 0)
    for g in range(F):
        values = [cells_ref[t, g] for t in range(NT)]
        total = time_sum(values)
        for t in range(NT):
            field = dissipation * values[t]
            at = t * F + g
            lower = jnp.where(layer == 0, before_ref[at : at + 1, :], pltpu.roll(field, 1, 0))
            upper = jnp.where(layer == LAYERS - 1, after_ref[at : at + 1, :], pltpu.roll(field, LAYERS - 1, 0))
            out_ref[t, g] = total[t] - (upper - 2.0 * field + lower)
    for t in range(NT):
        field = [cells_ref[t, f] for f in range(F)]
        for g in range(F):
            total = out_ref[t, g]
            for f in range(F):
                total = total + jac_ref[t, f, g].astype(f32) * field[f]
            out_ref[t, g] = total


def call(kernel, outs, args, flops=0, **more):
    size = sum(math.prod(a.shape) * a.dtype.itemsize for a in (*args, *jax.tree.leaves(outs)))
    return pl.pallas_call(
        kernel,
        out_shape=outs,
        compiler_params=pltpu.CompilerParams(vmem_limit_bytes=24 << 20),
        cost_estimate=pl.CostEstimate(flops=flops, bytes_accessed=size, transcendentals=0),
        **more,
    )(*args)


def body(adjoint_cells, flux_jacobian, dissipation, face_rows, owners, margin_weights, transposed_maps):
    cells = adjoint_cells[0].transpose(1, 2, 0, 3)
    jac = flux_jacobian[0].transpose(1, 2, 3, 0, 4)
    dissipation = dissipation[0]
    faces = face_rows.transpose(1, 2, 0, 3)
    owner = owners.transpose(2, 0, 1)
    margin = margin_weights.transpose(2, 0, 1)
    shape = jax.ShapeDtypeStruct

    maps = lax.all_gather(transposed_maps, SHARED, axis=0, tiled=True)
    outgoing = call(dispatch_kernel, shape((SLOTS, WIDTH), bf16), (faces, owner), 2 * SLOTS * 2 * ROWS * WIDTH)
    arrived = lax.all_to_all(outgoing.reshape(PEERS, SLOTS // PEERS, WIDTH), SPREAD, 0, 0, tiled=True)

    edge = shape((NT * F, NP), f32)
    lanes = 128
    first, last = call(
        edges_kernel,
        (edge, edge),
        (cells.reshape(NT * F * LAYERS, NP), dissipation),
        grid=(NP // lanes,),
        in_specs=[
            pl.BlockSpec((NT * F * LAYERS, lanes), lambda i: (0, i)),
            pl.BlockSpec((LAYERS, lanes), lambda i: (0, i)),
        ],
        out_specs=[pl.BlockSpec((NT * F, lanes), lambda i: (0, i))] * 2,
    )
    size = lax.axis_size(RADIAL)
    before = lax.ppermute(last, RADIAL, [(i, i + 1) for i in range(size - 1)])
    after = lax.ppermute(first, RADIAL, [(i + 1, i) for i in range(size - 1)])

    spread = shape((ROWS, SLOTS), bf16)
    high, low, time_faces = call(
        weights_kernel, (spread, spread, shape(faces.shape, f32)), (faces, owner, margin), 2 * ROWS * ROWS * SLOTS
    )

    products = call(
        maps_kernel, shape((PEERS, SLOTS // PEERS, WIDTH), bf16), (arrived, maps), 2 * SLOTS * F * 8 * FACE * FACE
    )
    returned = lax.all_to_all(products, SPREAD, 0, 0, tiled=True)

    cell_gradient = call(
        cells_kernel,
        shape(cells.shape, f32),
        (cells, jac, dissipation, before, after),
        24 * NT * F * LAYERS * NP,
        grid=(NP // lanes,),
        in_specs=[
            pl.BlockSpec((NT, F, LAYERS, lanes), lambda i: (0, 0, 0, i)),
            pl.BlockSpec((NT, F, F, LAYERS, lanes), lambda i: (0, 0, 0, 0, i)),
            pl.BlockSpec((LAYERS, lanes), lambda i: (0, i)),
            pl.BlockSpec((NT * F, lanes), lambda i: (0, i)),
            pl.BlockSpec((NT * F, lanes), lambda i: (0, i)),
        ],
        out_specs=pl.BlockSpec((NT, F, LAYERS, lanes), lambda i: (0, 0, 0, i)),
    )

    face_gradient = call(
        combine_kernel,
        shape(faces.shape, f32),
        (returned.reshape(SLOTS, WIDTH), high, low, time_faces),
        4 * ROWS * SLOTS * WIDTH,
    )
    return cell_gradient.transpose(2, 0, 1, 3)[None], face_gradient.transpose(2, 0, 1, 3)


def solution(mesh):
    chips = Mesh(mesh.devices.reshape(4, 4, 4, 2), ("x", "y", "z", "core"))
    every = ("x", "y", "z", "core")
    cells, faces = P("x", RADIAL), P(every)
    return jax.shard_map(
        body,
        mesh=chips,
        in_specs=(cells, cells, cells, faces, faces, faces, faces),
        out_specs=(cells, faces),
        check_vma=False,
    )
```

time: 110 us -> 84.8 us (0.77)
  the two profiles are of different devices: /device:TPU:22 before, /device:TPU:24 now
where the time goes in v1:
time: 84.8 us; the launch traced here: 84.3 us
  blocking collectives  24.6 us (29%)
  starting transfers between devices  14.7 us (17%)
  between operations  14.2 us (17%)
  Pallas kernels  12.3 us (15%)
  local copies, waits for them, and re-layouts  9.84 us (12%)
  waiting for transfers between devices  8.65 us (10%)
    all_to_all x1, blocking collectives, body(): lax.all_to_all(outgoing.reshape(PEERS, SLOTS // PEERS, WIDTH), SPREAD, 0,...  24.6 us
    pallas_call x6, Pallas kernels, call(): pl.pallas_call(kernel, out_shape=outs, compiler_params=pltpu.CompilerPara...  12.3 us
    unnamed x28, local copies, waits for them, and re-layouts  9.84 us
    ppermute x1, waiting for transfers between devices, body(): before = lax.ppermute(last, RADIAL, [(i, i + 1) for i in range(size - 1)])  7.97 us
    all_to_all x1, starting transfers between devices, body(): returned = lax.all_to_all(products, SPREAD, 0, 0, tiled=True)  6.97 us
    ppermute x1, starting transfers between devices, body(): after = lax.ppermute(first, RADIAL, [(i + 1, i) for i in range(size - 1)])  5.75 us
    ppermute x1, starting transfers between devices, body(): before = lax.ppermute(last, RADIAL, [(i, i + 1) for i in range(size - 1)])  1.92 us
  transfers between devices with their start and end apart: 4, of which 1 were waited for; matrix products, arithmetic and copies ran while one was open for 0% of the time, Pallas kernels for 9%

profile of v1, /device:TPU:24, one launch (start us, length us, event | category | flops | bytes accessed | tf_op | source)
XLA Modules:
  0.0 84.3 jit_solution(5574119296559597909)
XLA Ops:
  7.2 0.0 all-gather.2.cloned.1.call-start
  7.2 0.7 all-gather.2.cloned.1.call-update
  7.9 0.0 copy-start.3
  7.9 1.1 %copy-done.3 = f32[16,17,5,128]{3,0,2,1:T(8,128)S(1)} copy-done((f32[16,17,5,128]{3,0,2,1:T(8,128)S(1)}, f32[16,17,5,128]{3,0,2,1:T(8,128)}, u32[]{:S(2)}) %copy-start.3) | copy-done | bytes 696344
  9.0 0.7 copy-done.10
  9.7 1.4 %shard_map.88 = bf16[1024,640]{1,0:T(8,128)(2,1)S(1)} custom-call(f32[17,5,16,128]{3,2,1,0:T(8,128)S(1)} %bitcast.23, s32[3,16,17]{2,1,0:T(8,128)S(1)} %bitcast.27), custom_call_target="tpu_custom_call" | custom-call | flops 713031680 | bytes 2010304 | tf_op jit(solution)/shard_map/pallas_call | solution.py:158
  11.2 24.6 %all_to_all.10.rows_ref = bf16[16,64,640]{2,1,0:T(8,128)(2,1)S(1)} all-to-all(bf16[16,64,640]{2,1,0:T(8,128)(2,1)S(1)} %bitcast.22), channel_id=1, replica_groups=mesh['x'=4,'y'=4,'z'=4,'core'=2] {'x','y'}, dimensions={0} | all-to-all | bytes 2621440 | tf_op jit(solution)/shard_map/all_to_all | solution.py:178
  35.8 1.2 %copy-done.13 = bf16[32,128,128]{2,1,0:T(8,128)(2,1)S(1)} copy-done((bf16[32,128,128]{2,1,0:T(8,128)(2,1)S(1)}, bf16[32,128,128]{2,1,0:T(8,128)(2,1)}, u32[]{:S(2)}) %copy-start.13) | copy-done | bytes 1048600
  37.0 2.9 %shard_map.89 = bf16[16,64,640]{2,1,0:T(8,128)(2,1)S(1)} custom-call(bf16[16,64,640]{2,1,0:T(8,128)(2,1)S(1)} %all_to_all.10.rows_ref, bf16[32,128,128]{2,1,0:T(8,128)(2,1)S(1)} %copy-done.13), custom_call_target="tpu_custom_call" | custom-call | flops 1342177280 | bytes 3670016 | tf_op jit(solution)/shard_map/pallas_call | solution.py:158
  39.9 0.0 copy-start.2
  39.9 1.1 %copy-done.2 = bf16[16,64,640]{2,1,0:T(8,128)(2,1)} copy-done((bf16[16,64,640]{2,1,0:T(8,128)(2,1)}, bf16[16,64,640]{2,1,0:T(8,128)(2,1)S(1)}, u32[]{:S(2)}) %copy-start.2) | copy-done | bytes 1310744
  41.0 7.0 %all-to-all-start.1 = ((bf16[16,64,640]{2,1,0:T(8,128)(2,1)}), bf16[16,64,640]{2,1,0:T(8,128)(2,1)S(1)}, u32[]{:S(2)}, u32[]{:S(2)}) async-start(bf16[16,64,640]{2,1,0:T(8,128)(2,1)} %copy-done.2), calls=%async_computation.1 | async-start | bytes 2621440 | tf_op jit(solution)/shard_map/all_to_all | solution.py:205
  48.0 0.0 copy-start.11
  48.0 0.0 copy-start.12
  48.0 0.0 copy-done
  48.0 0.0 copy-done.9
  48.0 0.4 shard_map.86
  48.4 1.9 %collective-permute-start = (f32[85,512]{1,0:T(8,128)S(1)}, f32[85,512]{1,0:T(8,128)S(1)}, u32[]{:S(2)}, u32[]{:S(2)}) collective-permute-start(f32[85,512]{1,0:T(8,128)S(1)} %get-tuple-element.7), channel_id=1, source_target_pairs={{0,1},{1,2},{2,3},{3,4},{4,5},{5,6},{6,7},{7,8},{8,9},{9,10},{10,1... | collective-permute-start | bytes 522248 | tf_op jit(solution)/shard_map/ppermute | solution.py:194
  50.3 5.8 %collective-permute-start.1 = (f32[85,512]{1,0:T(8,128)S(1)}, f32[85,512]{1,0:T(8,128)S(1)}, u32[]{:S(2)}, u32[]{:S(2)}) collective-permute-start(f32[85,512]{1,0:T(8,128)S(1)} %get-tuple-element.8), channel_id=1, source_target_pairs={{1,0},{2,1},{3,2},{4,3},{5,4},{6,5},{7,6},{8,7},{9,8},{10,9},{11,1... | collective-permute-start | bytes 522248 | tf_op jit(solution)/shard_map/ppermute | solution.py:195
  56.1 0.0 copy-done.4
  56.1 2.0 %shard_map.90 = (bf16[272,1024]{1,0:T(8,128)(2,1)S(1)}, bf16[272,1024]{1,0:T(8,128)(2,1)S(1)}, f32[17,5,16,128]{3,2,1,0:T(8,128)S(1)}) custom-call(f32[17,5,16,128]{3,2,1,0:T(8,128)S(1)} %bitcast.24, s32[3,16,17]{2,1,0:T(8,128)S(1)} %bitcast.28, f32[3,16,17]{2,1,0:T(8,128)S(1)} %bitcast.29), custom_call_target="tpu_custom_call" | custom-call | flops 151519232 | bytes 2513280 | tf_op jit(solution)/shard_map/pallas_call | solution.py:158
  58.1 0.0 copy-start.5
  58.1 0.8 copy-done.5
  58.9 0.8 copy-done.7
  59.7 8.0 %collective-permute-done.before_ref = f32[85,512]{1,0:T(8,128)S(1)} collective-permute-done((f32[85,512]{1,0:T(8,128)S(1)}, f32[85,512]{1,0:T(8,128)S(1)}, u32[]{:S(2)}, u32[]{:S(2)}) %collective-permute-start) | collective-permute-done | bytes 174112 | tf_op jit(solution)/shard_map/ppermute | solution.py:194
  67.7 0.0 collective-permute-done.1.after_ref
  67.7 2.0 %copy-done.1 = bf16[1,8,17,5,5,512]{5,1,4,3,2,0:T(8,128)(2,1)S(1)} copy-done((bf16[1,8,17,5,5,512]{5,1,4,3,2,0:T(8,128)(2,1)S(1)}, bf16[1,8,17,5,5,512]{5,1,4,3,2,0:T(8,128)(2,1)}, u32[]{:S(2)}) %copy-start.1) | copy-done | bytes 3481624
  69.7 3.8 %shard_map.87 = f32[17,5,8,512]{3,2,1,0:T(8,128)} custom-call(f32[17,5,8,512]{3,2,1,0:T(8,128)S(1)} %bitcast.19, bf16[17,5,5,8,512]{4,3,2,1,0:T(8,128)(2,1)S(1)} %bitcast.21, f32[8,512]{1,0:T(8,128)S(1)} %bitcast.26, f32[85,512]{1,0:T(8,128)S(1)} %collective-permute-done.before_ref, f32[85,512]{1,0:T(8,128)S(1)} %collective-permute-done.1.after_ref), custom_call_target="tpu_custom_call" | custom-call | flops 8355840 | bytes 6631424 | tf_op jit(solution)/shard_map/pallas_call | solution.py:158
  73.4 0.0 all-to-all-done.1
  73.4 1.1 %copy-done.6 = bf16[272,1024]{1,0:T(8,128)(2,1)S(1)} copy-done((bf16[272,1024]{1,0:T(8,128)(2,1)S(1)}, bf16[272,1024]{1,0:T(8,128)(2,1)}, u32[]{:S(2)}) %copy-start.6) | copy-done | bytes 557080
  74.5 1.1 %copy-done.8 = bf16[272,1024]{1,0:T(8,128)(2,1)S(1)} copy-done((bf16[272,1024]{1,0:T(8,128)(2,1)S(1)}, bf16[272,1024]{1,0:T(8,128)(2,1)}, u32[]{:S(2)}) %copy-start.8) | copy-done | bytes 557080
  75.5 1.9 %shard_map.91 = f32[17,5,16,128]{3,2,1,0:T(8,128)} custom-call(bf16[1024,640]{1,0:T(8,128)(2,1)S(1)} %bitcast.20, bf16[272,1024]{1,0:T(8,128)(2,1)S(1)} %copy-done.6, bf16[272,1024]{1,0:T(8,128)(2,1)S(1)} %copy-done.8, f32[17,5,16,128]{3,2,1,0:T(8,128)S(1)} %get-tuple-element.11.time_ref), custom_call_target="tpu_custom_call" | custom-call | flops 713031680 | bytes 3817472 | tf_op jit(solution)/shard_map/pallas_call | solution.py:158
  (12 shorter events, 0.0 us)
Async XLA Ops:
  7.2 28.6 %all-gather.2.cloned.1.call-start = ((), (), s32[]{:S(2)}) async-start(), calls=%async_computation.2 | async-start | bytes 1179648 | tf_op jit(solution)/shard_map/all_gather | solution.py:176
  7.9 1.1 %copy-start.3 = (f32[16,17,5,128]{3,0,2,1:T(8,128)S(1)}, f32[16,17,5,128]{3,0,2,1:T(8,128)}, u32[]{:S(2)}) copy-start(f32[16,17,5,128]{3,0,2,1:T(8,128)} %param.10) | copy-start | bytes 2088964
  9.0 0.7 copy-start.10
  35.8 1.2 %copy-start.13 = (bf16[32,128,128]{2,1,0:T(8,128)(2,1)S(1)}, bf16[32,128,128]{2,1,0:T(8,128)(2,1)}, u32[]{:S(2)}) copy-start(bf16[32,128,128]{2,1,0:T(8,128)(2,1)} %all-gather.2.cloned.1.call-done.maps_ref) | copy-start | bytes 3145732
  39.9 1.1 %copy-start.2 = (bf16[16,64,640]{2,1,0:T(8,128)(2,1)}, bf16[16,64,640]{2,1,0:T(8,128)(2,1)S(1)}, u32[]{:S(2)}) copy-start(bf16[16,64,640]{2,1,0:T(8,128)(2,1)S(1)} %shard_map.89) | copy-start | bytes 3932164
  41.0 7.0 %copy-start = (f32[1,8,17,5,512]{4,1,3,2,0:T(8,128)S(1)}, f32[1,8,17,5,512]{4,1,3,2,0:T(8,128)}, u32[]{:S(2)}) copy-start(f32[1,8,17,5,512]{4,1,3,2,0:T(8,128)} %param.7) | copy-start | bytes 4177924
  41.0 7.0 %copy-start.9 = (f32[1,8,512]{2,1,0:T(8,128)S(1)}, f32[1,8,512]{2,1,0:T(8,128)}, u32[]{:S(2)}) copy-start(f32[1,8,512]{2,1,0:T(8,128)} %param.9) | copy-start | bytes 49156
  41.0 32.4 %all-to-all-start.1 = ((bf16[16,64,640]{2,1,0:T(8,128)(2,1)}), bf16[16,64,640]{2,1,0:T(8,128)(2,1)S(1)}, u32[]{:S(2)}, u32[]{:S(2)}) async-start(bf16[16,64,640]{2,1,0:T(8,128)(2,1)} %copy-done.2), calls=%async_computation.1 | async-start | bytes 2621440 | tf_op jit(solution)/shard_map/all_to_all | solution.py:205
  48.0 8.1 %copy-start.4 = (f32[16,17,5,128]{3,0,2,1:T(8,128)S(1)}, f32[16,17,5,128]{3,0,2,1:T(8,128)}, u32[]{:S(2)}) copy-start(f32[16,17,5,128]{3,0,2,1:T(8,128)} %param.10) | copy-start | bytes 2088964
  48.0 8.1 %copy-start.11 = (s32[16,17,3]{1,0,2:T(8,128)S(1)}, s32[16,17,3]{1,0,2:T(8,128)}, u32[]{:S(2)}) copy-start(s32[16,17,3]{1,0,2:T(8,128)} %param.11) | copy-start | bytes 9796
  48.0 8.1 %copy-start.12 = (f32[16,17,3]{1,0,2:T(8,128)S(1)}, f32[16,17,3]{1,0,2:T(8,128)}, u32[]{:S(2)}) copy-start(f32[16,17,3]{1,0,2:T(8,128)} %param.12) | copy-start | bytes 9796
  48.4 19.3 %collective-permute-start = (f32[85,512]{1,0:T(8,128)S(1)}, f32[85,512]{1,0:T(8,128)S(1)}, u32[]{:S(2)}, u32[]{:S(2)}) collective-permute-start(f32[85,512]{1,0:T(8,128)S(1)} %get-tuple-element.7), channel_id=1, source_target_pairs={{0,1},{1,2},{2,3},{3,4},{4,5},{5,6},{6,7},{7,8},{8,9},{9,10},{10,1... | collective-permute-start | bytes 522248 | tf_op jit(solution)/shard_map/ppermute | solution.py:194
  50.3 17.3 %collective-permute-start.1 = (f32[85,512]{1,0:T(8,128)S(1)}, f32[85,512]{1,0:T(8,128)S(1)}, u32[]{:S(2)}, u32[]{:S(2)}) collective-permute-start(f32[85,512]{1,0:T(8,128)S(1)} %get-tuple-element.8), channel_id=1, source_target_pairs={{1,0},{2,1},{3,2},{4,3},{5,4},{6,5},{7,6},{8,7},{9,8},{10,9},{11,1... | collective-permute-start | bytes 522248 | tf_op jit(solution)/shard_map/ppermute | solution.py:195
  58.1 0.8 copy-start.5
  58.9 0.8 copy-start.7
  67.7 2.0 %copy-start.1 = (bf16[1,8,17,5,5,512]{5,1,4,3,2,0:T(8,128)(2,1)S(1)}, bf16[1,8,17,5,5,512]{5,1,4,3,2,0:T(8,128)(2,1)}, u32[]{:S(2)}) copy-start(bf16[1,8,17,5,5,512]{5,1,4,3,2,0:T(8,128)(2,1)} %param.8) | copy-start | bytes 10444804
  73.4 1.1 %copy-start.6 = (bf16[272,1024]{1,0:T(8,128)(2,1)S(1)}, bf16[272,1024]{1,0:T(8,128)(2,1)}, u32[]{:S(2)}) copy-start(bf16[272,1024]{1,0:T(8,128)(2,1)} %copy-done.5) | copy-start | bytes 1671172
  74.5 1.1 %copy-start.8 = (bf16[272,1024]{1,0:T(8,128)(2,1)S(1)}, bf16[272,1024]{1,0:T(8,128)(2,1)}, u32[]{:S(2)}) copy-start(bf16[272,1024]{1,0:T(8,128)(2,1)} %copy-done.7) | copy-start | bytes 1671172
Sparse Core Ops, SparseCore 0:
  9.7 25.6 all-gather.1

commit v2 on v1

--- a/solution.py
+++ b/solution.py
@@ -26,7 +26,8 @@
 GROUP = BLOCKS // PEERS
 
 SPREAD = ("x", "y")
-SHARED = ("z", "core")
+STEPS = (0, 1, 3, 2)
+PARTS = 4
 RADIAL = ("y", "z", "core")
 f32 = jnp.float32
 bf16 = jnp.bfloat16
@@ -61,25 +62,38 @@
     return jnp.sum(jnp.where(col % TILES == sub, spread, 0.0), axis=1)
 
 
-def dispatch_kernel(face_ref, owner_ref, out_ref):
+def dispatch_kernel(face_hbm, owner_hbm, out_hbm, face_ref, owner_ref, out_ref, face_sem, owner_sem, out_sem):
+    owner_copy = pltpu.make_async_copy(owner_hbm, owner_ref, owner_sem)
+    face_copy = pltpu.make_async_copy(face_hbm, face_ref, face_sem)
+    owner_copy.start()
+    face_copy.start()
+    earlier = lax.broadcasted_iota(jnp.int32, (ROWS, ROWS), 0) < lax.broadcasted_iota(
+        jnp.int32, (ROWS, ROWS), 1
+    )
+    earlier = jnp.where(earlier, 1.0, 0.0).astype(bf16)
+    block = lax.broadcasted_iota(jnp.int32, (BLOCKS, ROWS), 0)
+    owner_copy.wait()
     owner = lane_rows(owner_ref).astype(jnp.int32)
-    block = lax.broadcasted_iota(jnp.int32, (BLOCKS, ROWS), 0)
     hit = (owner[0:1] == block) | (owner[1:2] == block) | (owner[2:3] == block)
     hit = jnp.where(hit, 1.0, 0.0)
-    earlier = lax.broadcasted_iota(jnp.int32, (ROWS, ROWS), 0) < lax.broadcasted_iota(
-        jnp.int32, (ROWS, ROWS), 1
-    )
-    earlier = jnp.where(earlier, 1.0, 0.0).astype(bf16)
     rank = jnp.dot(hit.astype(bf16), earlier, preferred_element_type=f32)
     first = jnp.where(rank < 0.5, hit, 0.0).reshape(BLOCKS // 8, 8, ROWS)
     second = jnp.where(rank > 0.5, hit, 0.0).reshape(BLOCKS // 8, 8, ROWS)
     select = jnp.stack([first, second], axis=1).reshape(SLOTS, ROWS).astype(bf16)
+    face_copy.wait()
     rows = [face_ref[:, f].reshape(ROWS, FACE).astype(bf16) for f in range(F)]
     rows = jnp.concatenate(rows, axis=1)
-    out_ref[...] = jnp.dot(select, rows, preferred_element_type=f32).astype(bf16)
-
-
-def weights_kernel(face_ref, owner_ref, margin_ref, high_ref, low_ref, time_ref):
+    copies = []
+    for part in range(PARTS):
+        piece = slice(part * SLOTS // PARTS, (part + 1) * SLOTS // PARTS)
+        out_ref[piece] = jnp.dot(select[piece], rows, preferred_element_type=f32).astype(bf16)
+        copies.append(pltpu.make_async_copy(out_ref.at[piece], out_hbm.at[piece], out_sem.at[part]))
+        copies[-1].start()
+    for copy in copies:
+        copy.wait()
+
+
+def weights_kernel(face_ref, owner_ref, margin_ref, weight_ref, time_ref):
     both = jnp.concatenate([lane_rows(owner_ref), lane_rows(margin_ref), jnp.zeros((2, ROWS), f32)], axis=0)
     both = both.T
     slot = lax.broadcasted_iota(jnp.int32, (ROWS, SLOTS), 1)
@@ -98,32 +112,69 @@
     own = (slot // 8 % 2).astype(f32)
     weight = jnp.where(jnp.abs(rank - own) < 0.5, weight, 0.0)
     high = weight.astype(bf16)
-    high_ref[...] = high
-    low_ref[...] = (weight - high.astype(f32)).astype(bf16)
+    weight_ref[0] = high
+    weight_ref[1] = (weight - high.astype(f32)).astype(bf16)
     for f in range(F):
         total = time_sum([face_ref[t, f] for t in range(NT)])
         for t in range(NT):
             time_ref[t, f] = total[t]
 
 
-def maps_kernel(rows_ref, maps_ref, out_ref):
-    sub = lax.broadcasted_iota(jnp.int32, (PEERS, 16, FACE), 1) % 8
-    for g in range(GROUP // 8):
-        maps = maps_ref[8 * g : 8 * g + 8].reshape(8 * FACE, FACE)
+def maps_kernel(rows_ref, *refs):
+    pieces, (out_hbm, maps_ref, out_ref, maps_sem, out_sem) = refs[:8], refs[-5:]
+    z, core = lax.axis_index("z"), lax.axis_index("core")
+    loads = []
+    for d in range(4):
+        loads.append([pltpu.make_async_copy(pieces[2 * d + i], maps_ref.at[d, i], maps_sem.at[d, i]) for i in range(2)])
+        for load in loads[d]:
+            load.start()
+    sub = lax.broadcasted_iota(jnp.int32, (16, FACE), 0)
+    masks = [jnp.where(sub % 4 == q, 1.0, 0.0).astype(bf16) for q in range(4)]
+    near = sub % 8 // 4 == core
+    stores = []
+    for d, step in enumerate(STEPS):
+        span = pl.ds(pl.multiple_of((z + (4 - step)) % 4 * 16, 16), 16)
+        for load in loads[d]:
+            load.wait()
+        maps = [maps_ref[d, i].reshape(4 * FACE, FACE) for i in range(2)]
+        maps = jnp.concatenate(maps, axis=1)
         for f in range(F):
             lanes = slice(f * FACE, (f + 1) * FACE)
-            rows = rows_ref[:, 16 * g : 16 * g + 16, lanes].astype(f32)
-            parts = [jnp.where(sub == q, rows, 0.0).reshape(PEERS * 16, FACE).astype(bf16) for q in range(8)]
+            rows = rows_ref[:, span, lanes]
+            parts = [(rows * mask).reshape(PEERS * 16, FACE) for mask in masks]
             result = jnp.dot(jnp.concatenate(parts, axis=1), maps, preferred_element_type=f32)
-            out_ref[:, 16 * g : 16 * g + 16, lanes] = result.astype(bf16).reshape(PEERS, 16, FACE)
-
-
-def combine_kernel(rows_ref, high_ref, low_ref, time_ref, out_ref):
-    rows = rows_ref[...]
-    total = jnp.dot(high_ref[...], rows, preferred_element_type=f32)
-    total = total + jnp.dot(low_ref[...], rows, preferred_element_type=f32)
-    for f in range(F):
-        out_ref[:, f] = time_ref[:, f] + total[:, f * FACE : (f + 1) * FACE].reshape(NT, TILES, FACE)
+            result = result.reshape(PEERS, 16, 2 * FACE)
+            out_ref[d, :, :, lanes] = jnp.where(near, result[..., :FACE], result[..., FACE:]).astype(bf16)
+        stores.append(pltpu.make_async_copy(out_ref.at[d], out_hbm.at[:, span], out_sem.at[d]))
+        stores[d].start()
+    for store in stores:
+        store.wait()
+
+
+def combine_kernel(rows_ref, weight_hbm, time_hbm, out_hbm, weight_ref, time_ref, out_ref, in_sem, out_sem):
+    loads = [pltpu.make_async_copy(weight_hbm.at[i], weight_ref.at[i], in_sem.at[i]) for i in range(2)]
+    loads.append(pltpu.make_async_copy(time_hbm, time_ref, in_sem.at[2]))
+    for load in loads:
+        load.start()
+    stores = []
+    for i, fields in enumerate(((0, 1), (2, 3), (4,))):
+        rows = rows_ref[:, fields[0] * FACE : (fields[-1] + 1) * FACE]
+        total = None
+        for part in range(2):
+            if i == 0:
+                loads[part].wait()
+            term = jnp.dot(weight_ref[part], rows, preferred_element_type=f32)
+            total = term if total is None else total + term
+        if i == 0:
+            loads[2].wait()
+        for j, f in enumerate(fields):
+            part = total[:, j * FACE : (j + 1) * FACE].reshape(NT, TILES, FACE)
+            out_ref[:, f] = time_ref[:, f] + part
+        span = pl.ds(fields[0], len(fields))
+        stores.append(pltpu.make_async_copy(out_ref.at[:, span], out_hbm.at[:, span], out_sem.at[i]))
+        stores[-1].start()
+    for store in stores:
+        store.wait()
 
 
 def edges_kernel(cells_ref, dissipation_ref, first_ref, last_ref):
@@ -153,6 +204,14 @@
             out_ref[t, g] = total
 
 
+def in_hbm(*values):
+    return tuple(pltpu.with_memory_space_constraint(v, pltpu.HBM) for v in values)
+
+
+def in_vmem(value):
+    return pltpu.with_memory_space_constraint(value, pltpu.VMEM)
+
+
 def call(kernel, outs, args, flops=0, **more):
     size = sum(math.prod(a.shape) * a.dtype.itemsize for a in (*args, *jax.tree.leaves(outs)))
     return pl.pallas_call(
@@ -164,6 +223,11 @@
     )(*args)
 
 
+def shift(value, axis, step):
+    size = lax.axis_size(axis)
+    return lax.ppermute(value, axis, [(i, (i + step) % size) for i in range(size)])
+
+
 def body(adjoint_cells, flux_jacobian, dissipation, face_rows, owners, margin_weights, transposed_maps):
     cells = adjoint_cells[0].transpose(1, 2, 0, 3)
     jac = flux_jacobian[0].transpose(1, 2, 3, 0, 4)
@@ -172,17 +236,39 @@
     owner = owners.transpose(2, 0, 1)
     margin = margin_weights.transpose(2, 0, 1)
     shape = jax.ShapeDtypeStruct
-
-    maps = lax.all_gather(transposed_maps, SHARED, axis=0, tiled=True)
-    outgoing = call(dispatch_kernel, shape((SLOTS, WIDTH), bf16), (faces, owner), 2 * SLOTS * 2 * ROWS * WIDTH)
+    hbm = pl.BlockSpec(memory_space=pltpu.HBM)
+    vmem = pl.BlockSpec(memory_space=pltpu.VMEM)
+    dma = pltpu.SemaphoreType.DMA
+
+    outgoing = call(
+        dispatch_kernel,
+        pltpu.HBM((SLOTS, WIDTH), bf16),
+        in_hbm(faces, owner),
+        2 * SLOTS * 2 * ROWS * WIDTH,
+        in_specs=[hbm, hbm],
+        out_specs=hbm,
+        scratch_shapes=[
+            pltpu.VMEM(faces.shape, f32),
+            pltpu.VMEM(owner.shape, jnp.int32),
+            pltpu.VMEM((SLOTS, WIDTH), bf16),
+            dma,
+            dma,
+            dma((PARTS,)),
+        ],
+    )
     arrived = lax.all_to_all(outgoing.reshape(PEERS, SLOTS // PEERS, WIDTH), SPREAD, 0, 0, tiled=True)
+
+    pieces = []
+    for step in STEPS:
+        piece = shift(transposed_maps, "z", step) if step else transposed_maps
+        pieces += [piece, shift(piece, "core", 1)]
 
     edge = shape((NT * F, NP), f32)
     lanes = 128
     first, last = call(
         edges_kernel,
         (edge, edge),
-        (cells.reshape(NT * F * LAYERS, NP), dissipation),
+        in_hbm(cells.reshape(NT * F * LAYERS, NP), dissipation),
         grid=(NP // lanes,),
         in_specs=[
             pl.BlockSpec((NT * F * LAYERS, lanes), lambda i: (0, i)),
@@ -194,20 +280,34 @@
     before = lax.ppermute(last, RADIAL, [(i, i + 1) for i in range(size - 1)])
     after = lax.ppermute(first, RADIAL, [(i + 1, i) for i in range(size - 1)])
 
-    spread = shape((ROWS, SLOTS), bf16)
-    high, low, time_faces = call(
-        weights_kernel, (spread, spread, shape(faces.shape, f32)), (faces, owner, margin), 2 * ROWS * ROWS * SLOTS
-    )
-
+    weights, time_faces = call(
+        weights_kernel,
+        (pltpu.HBM((2, ROWS, SLOTS), bf16), pltpu.HBM(faces.shape, f32)),
+        in_hbm(faces, owner, margin),
+        2 * ROWS * ROWS * SLOTS,
+    )
+
+    before, after = in_hbm(before, after)
     products = call(
-        maps_kernel, shape((PEERS, SLOTS // PEERS, WIDTH), bf16), (arrived, maps), 2 * SLOTS * F * 8 * FACE * FACE
+        maps_kernel,
+        pltpu.HBM((PEERS, SLOTS // PEERS, WIDTH), bf16),
+        (in_vmem(arrived), *in_hbm(*pieces), before, after),
+        2 * SLOTS * F * 8 * FACE * FACE,
+        in_specs=[vmem] + [hbm] * 10,
+        out_specs=hbm,
+        scratch_shapes=[
+            pltpu.VMEM((4, 2, 4, FACE, FACE), bf16),
+            pltpu.VMEM((4, PEERS, 16, WIDTH), bf16),
+            dma((4, 2)),
+            dma((4,)),
+        ],
     )
     returned = lax.all_to_all(products, SPREAD, 0, 0, tiled=True)
 
     cell_gradient = call(
         cells_kernel,
-        shape(cells.shape, f32),
-        (cells, jac, dissipation, before, after),
+        pltpu.HBM(cells.shape, f32),
+        in_hbm(cells, jac, dissipation, before, after),
         24 * NT * F * LAYERS * NP,
         grid=(NP // lanes,),
         in_specs=[
@@ -222,9 +322,18 @@
 
     face_gradient = call(
         combine_kernel,
-        shape(faces.shape, f32),
-        (returned.reshape(SLOTS, WIDTH), high, low, time_faces),
+        pltpu.HBM(faces.shape, f32),
+        (in_vmem(returned.reshape(SLOTS, WIDTH)), *in_hbm(weights, time_faces)),
         4 * ROWS * SLOTS * WIDTH,
+        in_specs=[vmem, hbm, hbm],
+        out_specs=hbm,
+        scratch_shapes=[
+            pltpu.VMEM((2, ROWS, SLOTS), bf16),
+            pltpu.VMEM(faces.shape, f32),
+            pltpu.VMEM(faces.shape, f32),
+            dma((3,)),
+            dma((3,)),
+        ],
     )
     return cell_gradient.transpose(2, 0, 1, 3)[None], face_gradient.transpose(2, 0, 1, 3)
 

time: 84.8 us -> 66.7 us (0.79)
  the two profiles are of different devices: /device:TPU:24 before, /device:TPU:0 now
where the time goes in v2:
time: 66.7 us; the launch traced here: 66.2 us
  starting transfers between devices  27.9 us (42%)
  Pallas kernels  22.2 us (33%)
  waiting for transfers between devices  15.2 us (23%)
  between operations  0.8 us (1%)
    pallas_call x6, Pallas kernels, call(): pl.pallas_call(kernel, out_shape=outs, compiler_params=pltpu.CompilerPara...  22.2 us
    all_to_all x1, starting transfers between devices, body(): returned = lax.all_to_all(products, SPREAD, 0, 0, tiled=True)  9.12 us
    all_to_all x1, waiting for transfers between devices, body(): returned = lax.all_to_all(products, SPREAD, 0, 0, tiled=True)  8.25 us
    ppermute x7, starting transfers between devices, shift(): lax.ppermute(value, axis, [(i, (i + step) % size) for i in range(size)])  7.82 us
    all_to_all x1, starting transfers between devices, body(): lax.all_to_all(outgoing.reshape(PEERS, SLOTS // PEERS, WIDTH), SPREAD, 0,...  7.26 us
    all_to_all x1, waiting for transfers between devices, body(): lax.all_to_all(outgoing.reshape(PEERS, SLOTS // PEERS, WIDTH), SPREAD, 0,...  5.96 us
    ppermute x1, starting transfers between devices, body(): before = lax.ppermute(last, RADIAL, [(i, i + 1) for i in range(size - 1)])  2.42 us
  transfers between devices with their start and end apart: 11, of which 6 were waited for; matrix products, arithmetic and copies ran while one was open for 0% of the time, Pallas kernels for 17%

profile of v2, /device:TPU:0, one launch (start us, length us, event | category | flops | bytes accessed | tf_op | source)
XLA Modules:
  0.0 66.2 jit_solution(16563549751773968811)
XLA Ops:
  0.6 3.1 %shard_map.88 = bf16[1024,640]{1,0:T(8,128)(2,1)} custom-call(f32[17,5,16,128]{3,2,1,0:T(8,128)} %bitcast.24, s32[3,16,17]{2,1,0:T(8,128)} %bitcast.29), custom_call_target="tpu_custom_call" | custom-call | flops 713031680 | bytes 2010304 | tf_op jit(solution)/shard_map/pallas_call | solution.py:217
  3.8 0.0 copy-start.2
  3.8 7.3 %all-to-all-start = ((bf16[16,64,640]{2,1,0:T(8,128)(2,1)}), bf16[16,64,640]{2,1,0:T(8,128)(2,1)S(1)}, u32[]{:S(2)}, u32[]{:S(2)}) async-start(bf16[16,64,640]{2,1,0:T(8,128)(2,1)} %bitcast.23), calls=%async_computation | async-start | bytes 2621440 | tf_op jit(solution)/shard_map/all_to_all | solution.py:259
  11.0 0.0 copy-done.2
  11.0 2.0 %collective-permute-start.3 = (bf16[4,128,128]{2,1,0:T(8,128)(2,1)S(1)}, bf16[4,128,128]{2,1,0:T(8,128)(2,1)S(1)}, u32[]{:S(2)}, u32[]{:S(2)}) collective-permute-start(bf16[4,128,128]{2,1,0:T(8,128)(2,1)S(1)} %copy-done.2), channel_id=1, source_target_pairs={{0,2},{2,4},{4,6},{6,0},{1,3},{3,5},{5,7},{7,1},{8,10},{10,12},{12... | collective-permute-start | bytes 393224 | tf_op jit(solution)/shard_map/ppermute | solution.py:228
  13.0 2.2 %collective-permute-start.5 = (bf16[4,128,128]{2,1,0:T(8,128)(2,1)S(1)}, bf16[4,128,128]{2,1,0:T(8,128)(2,1)S(1)}, u32[]{:S(2)}, u32[]{:S(2)}) collective-permute-start(bf16[4,128,128]{2,1,0:T(8,128)(2,1)S(1)} %copy-done.2), channel_id=1, source_target_pairs={{0,6},{2,0},{4,2},{6,4},{1,7},{3,1},{5,3},{7,5},{8,14},{10,8},{12,... | collective-permute-start | bytes 393224 | tf_op jit(solution)/shard_map/ppermute | solution.py:228
  15.2 1.8 %collective-permute-start.7 = (bf16[4,128,128]{2,1,0:T(8,128)(2,1)S(1)}, bf16[4,128,128]{2,1,0:T(8,128)(2,1)S(1)}, u32[]{:S(2)}, u32[]{:S(2)}) collective-permute-start(bf16[4,128,128]{2,1,0:T(8,128)(2,1)S(1)} %copy-done.2), channel_id=1, source_target_pairs={{0,4},{2,6},{4,0},{6,2},{1,5},{3,7},{5,1},{7,3},{8,12},{10,14},{12... | collective-permute-start | bytes 393224 | tf_op jit(solution)/shard_map/ppermute | solution.py:228
  17.0 0.0 collective-permute-start.2
  17.0 2.2 %shard_map.86 = (f32[85,512]{1,0:T(8,128)S(1)}, f32[85,512]{1,0:T(8,128)S(1)}) custom-call(f32[680,512]{1,0:T(8,128)} %bitcast.19, f32[8,512]{1,0:T(8,128)} %bitcast.27), custom_call_target="tpu_custom_call" | custom-call | bytes 1757184 | tf_op jit(solution)/shard_map/pallas_call | solution.py:217
  19.2 2.4 %collective-permute-start = (f32[85,512]{1,0:T(8,128)S(1)}, f32[85,512]{1,0:T(8,128)S(1)}, u32[]{:S(2)}, u32[]{:S(2)}) collective-permute-start(f32[85,512]{1,0:T(8,128)S(1)} %get-tuple-element.6), channel_id=1, source_target_pairs={{0,1},{1,2},{2,3},{3,4},{4,5},{5,6},{6,7},{7,8},{8,9},{9,10},{10,1... | collective-permute-start | bytes 522248 | tf_op jit(solution)/shard_map/ppermute | solution.py:280
  21.6 0.0 collective-permute-done.3.refs_2_
  21.7 0.0 copy-start.3
  21.7 1.3 %collective-permute-start.1 = (f32[85,512]{1,0:T(8,128)S(1)}, f32[85,512]{1,0:T(8,128)S(1)}, u32[]{:S(2)}, u32[]{:S(2)}) collective-permute-start(f32[85,512]{1,0:T(8,128)S(1)} %get-tuple-element.7), channel_id=1, source_target_pairs={{1,0},{2,1},{3,2},{4,3},{5,4},{6,5},{7,6},{8,7},{9,8},{10,9},{11,1... | collective-permute-start | bytes 522248 | tf_op jit(solution)/shard_map/ppermute | solution.py:281
  23.0 0.0 collective-permute-done.5.refs_4_
  23.0 0.0 copy-start.4
  23.0 1.3 %collective-permute-start.4 = (bf16[4,128,128]{2,1,0:T(8,128)(2,1)S(1)}, bf16[4,128,128]{2,1,0:T(8,128)(2,1)S(1)}, u32[]{:S(2)}, u32[]{:S(2)}) collective-permute-start(bf16[4,128,128]{2,1,0:T(8,128)(2,1)S(1)} %collective-permute-done.3.refs_2_), channel_id=1, source_target_pairs={{0,1},{1,0},{2,3},{3,2},{4,5},{5,4},{6,7},{7,6},{8,9},{9,8},{10,11... | collective-permute-start | bytes 393224 | tf_op jit(solution)/shard_map/ppermute | solution.py:228
  24.3 0.0 collective-permute-done.7.refs_6_
  24.3 0.1 collective-permute-start.6
  24.4 0.0 collective-permute-done.2.refs_1_
  24.4 0.4 collective-permute-start.8
  24.8 0.0 collective-permute-done.before_ref.refs_8_
  24.8 0.3 collective-permute-done.1.after_ref.refs_9_
  25.1 0.2 collective-permute-done.4.refs_3_
  25.3 0.4 collective-permute-done.6.refs_5_
  25.7 0.2 collective-permute-done.8.refs_7_
  25.9 6.0 %all-to-all-done.rows_ref = bf16[16,64,640]{2,1,0:T(8,128)(2,1)S(1)} async-done(((bf16[16,64,640]{2,1,0:T(8,128)(2,1)}), bf16[16,64,640]{2,1,0:T(8,128)(2,1)S(1)}, u32[]{:S(2)}, u32[]{:S(2)}) %all-to-all-start) | async-done | bytes 1310752 | tf_op jit(solution)/shard_map/all_to_all | solution.py:259
  31.9 4.2 %shard_map.89 = bf16[16,64,640]{2,1,0:T(8,128)(2,1)} custom-call(bf16[16,64,640]{2,1,0:T(8,128)(2,1)S(1)} %all-to-all-done.rows_ref, bf16[4,128,128]{2,1,0:T(8,128)(2,1)} %refs_0_.1, bf16[4,128,128]{2,1,0:T(8,128)(2,1)} %copy-done.6, bf16[4,128,128]{2,1,0:T(8,128)(2,1)} %copy-done.3, bf16[4,128,128]{2,1,0:T(8,128)(2,1)} %copy-done.7, ...), custom_call_target="tpu_custom_call" | custom-call | flops 1342177280 | bytes 4018176 | tf_op jit(solution)/shard_map/pallas_call | solution.py:217
  36.1 9.1 %all-to-all-start.1 = ((bf16[16,64,640]{2,1,0:T(8,128)(2,1)}), bf16[16,64,640]{2,1,0:T(8,128)(2,1)S(1)}, u32[]{:S(2)}, u32[]{:S(2)}) async-start(bf16[16,64,640]{2,1,0:T(8,128)(2,1)} %shard_map.89), calls=%async_computation.1 | async-start | bytes 2621440 | tf_op jit(solution)/shard_map/all_to_all | solution.py:305
  45.2 3.9 %shard_map.90 = (bf16[2,272,1024]{2,1,0:T(8,128)(2,1)}, f32[17,5,16,128]{3,2,1,0:T(8,128)}) custom-call(f32[17,5,16,128]{3,2,1,0:T(8,128)} %bitcast.25, s32[3,16,17]{2,1,0:T(8,128)} %bitcast.30, f32[3,16,17]{2,1,0:T(8,128)} %bitcast.31), custom_call_target="tpu_custom_call" | custom-call | flops 151519232 | bytes 2513280 | tf_op jit(solution)/shard_map/pallas_call | solution.py:217
  49.1 5.2 %shard_map.87 = f32[17,5,8,512]{3,2,1,0:T(8,128)} custom-call(f32[17,5,8,512]{3,2,1,0:T(8,128)} %bitcast.20, bf16[17,5,5,8,512]{4,3,2,1,0:T(8,128)(2,1)} %bitcast.21, f32[8,512]{1,0:T(8,128)} %bitcast.28, f32[85,512]{1,0:T(8,128)} %copy-done, f32[85,512]{1,0:T(8,128)} %copy-done.1), custom_call_target="tpu_custom_call" | custom-call | flops 8355840 | bytes 6631424 | tf_op jit(solution)/shard_map/pallas_call | solution.py:217
  54.3 8.2 %all-to-all-done.1 = bf16[16,64,640]{2,1,0:T(8,128)(2,1)S(1)} async-done(((bf16[16,64,640]{2,1,0:T(8,128)(2,1)}), bf16[16,64,640]{2,1,0:T(8,128)(2,1)S(1)}, u32[]{:S(2)}, u32[]{:S(2)}) %all-to-all-start.1) | async-done | bytes 1310752 | tf_op jit(solution)/shard_map/all_to_all | solution.py:305
  62.5 3.7 %shard_map.91 = f32[17,5,16,128]{3,2,1,0:T(8,128)} custom-call(bf16[1024,640]{1,0:T(8,128)(2,1)S(1)} %bitcast.18, bf16[2,272,1024]{2,1,0:T(8,128)(2,1)} %get-tuple-element.8.weight_hbm, f32[17,5,16,128]{3,2,1,0:T(8,128)} %get-tuple-element.9.time_hbm), custom_call_target="tpu_custom_call" | custom-call | flops 713031680 | bytes 3817472 | tf_op jit(solution)/shard_map/pallas_call | solution.py:217
  (16 shorter events, 0.0 us)
Async XLA Ops:
  3.8 7.3 %copy-start.2 = (bf16[4,128,128]{2,1,0:T(8,128)(2,1)S(1)}, bf16[4,128,128]{2,1,0:T(8,128)(2,1)}, u32[]{:S(2)}) copy-start(bf16[4,128,128]{2,1,0:T(8,128)(2,1)} %refs_0_.1) | copy-start | bytes 393220
  3.8 28.1 %all-to-all-start = ((bf16[16,64,640]{2,1,0:T(8,128)(2,1)}), bf16[16,64,640]{2,1,0:T(8,128)(2,1)S(1)}, u32[]{:S(2)}, u32[]{:S(2)}) async-start(bf16[16,64,640]{2,1,0:T(8,128)(2,1)} %bitcast.23), calls=%async_computation | async-start | bytes 2621440 | tf_op jit(solution)/shard_map/all_to_all | solution.py:259
  11.0 10.6 %collective-permute-start.3 = (bf16[4,128,128]{2,1,0:T(8,128)(2,1)S(1)}, bf16[4,128,128]{2,1,0:T(8,128)(2,1)S(1)}, u32[]{:S(2)}, u32[]{:S(2)}) collective-permute-start(bf16[4,128,128]{2,1,0:T(8,128)(2,1)S(1)} %copy-done.2), channel_id=1, source_target_pairs={{0,2},{2,4},{4,6},{6,0},{1,3},{3,5},{5,7},{7,1},{8,10},{10,12},{12... | collective-permute-start | bytes 393224 | tf_op jit(solution)/shard_map/ppermute | solution.py:228
  13.0 9.9 %collective-permute-start.5 = (bf16[4,128,128]{2,1,0:T(8,128)(2,1)S(1)}, bf16[4,128,128]{2,1,0:T(8,128)(2,1)S(1)}, u32[]{:S(2)}, u32[]{:S(2)}) collective-permute-start(bf16[4,128,128]{2,1,0:T(8,128)(2,1)S(1)} %copy-done.2), channel_id=1, source_target_pairs={{0,6},{2,0},{4,2},{6,4},{1,7},{3,1},{5,3},{7,5},{8,14},{10,8},{12,... | collective-permute-start | bytes 393224 | tf_op jit(solution)/shard_map/ppermute | solution.py:228
  15.2 9.1 %collective-permute-start.7 = (bf16[4,128,128]{2,1,0:T(8,128)(2,1)S(1)}, bf16[4,128,128]{2,1,0:T(8,128)(2,1)S(1)}, u32[]{:S(2)}, u32[]{:S(2)}) collective-permute-start(bf16[4,128,128]{2,1,0:T(8,128)(2,1)S(1)} %copy-done.2), channel_id=1, source_target_pairs={{0,4},{2,6},{4,0},{6,2},{1,5},{3,7},{5,1},{7,3},{8,12},{10,14},{12... | collective-permute-start | bytes 393224 | tf_op jit(solution)/shard_map/ppermute | solution.py:228
  17.0 7.4 %collective-permute-start.2 = (bf16[4,128,128]{2,1,0:T(8,128)(2,1)S(1)}, bf16[4,128,128]{2,1,0:T(8,128)(2,1)S(1)}, u32[]{:S(2)}, u32[]{:S(2)}) collective-permute-start(bf16[4,128,128]{2,1,0:T(8,128)(2,1)S(1)} %copy-done.2), channel_id=1, source_target_pairs={{0,1},{1,0},{2,3},{3,2},{4,5},{5,4},{6,7},{7,6},{8,9},{9,8},{10,11... | collective-permute-start | bytes 393224 | tf_op jit(solution)/shard_map/ppermute | solution.py:228
  19.2 5.6 %collective-permute-start = (f32[85,512]{1,0:T(8,128)S(1)}, f32[85,512]{1,0:T(8,128)S(1)}, u32[]{:S(2)}, u32[]{:S(2)}) collective-permute-start(f32[85,512]{1,0:T(8,128)S(1)} %get-tuple-element.6), channel_id=1, source_target_pairs={{0,1},{1,2},{2,3},{3,4},{4,5},{5,6},{6,7},{7,8},{8,9},{9,10},{10,1... | collective-permute-start | bytes 522248 | tf_op jit(solution)/shard_map/ppermute | solution.py:280
  21.7 10.2 %copy-start.3 = (bf16[4,128,128]{2,1,0:T(8,128)(2,1)}, bf16[4,128,128]{2,1,0:T(8,128)(2,1)S(1)}, u32[]{:S(2)}) copy-start(bf16[4,128,128]{2,1,0:T(8,128)(2,1)S(1)} %collective-permute-done.3.refs_2_) | copy-start | bytes 393220
  21.7 3.4 %collective-permute-start.1 = (f32[85,512]{1,0:T(8,128)S(1)}, f32[85,512]{1,0:T(8,128)S(1)}, u32[]{:S(2)}, u32[]{:S(2)}) collective-permute-start(f32[85,512]{1,0:T(8,128)S(1)} %get-tuple-element.7), channel_id=1, source_target_pairs={{1,0},{2,1},{3,2},{4,3},{5,4},{6,5},{7,6},{8,7},{9,8},{10,9},{11,1... | collective-permute-start | bytes 522248 | tf_op jit(solution)/shard_map/ppermute | solution.py:281
  23.0 8.9 %copy-start.4 = (bf16[4,128,128]{2,1,0:T(8,128)(2,1)}, bf16[4,128,128]{2,1,0:T(8,128)(2,1)S(1)}, u32[]{:S(2)}) copy-start(bf16[4,128,128]{2,1,0:T(8,128)(2,1)S(1)} %collective-permute-done.5.refs_4_) | copy-start | bytes 393220
  23.0 2.3 %collective-permute-start.4 = (bf16[4,128,128]{2,1,0:T(8,128)(2,1)S(1)}, bf16[4,128,128]{2,1,0:T(8,128)(2,1)S(1)}, u32[]{:S(2)}, u32[]{:S(2)}) collective-permute-start(bf16[4,128,128]{2,1,0:T(8,128)(2,1)S(1)} %collective-permute-done.3.refs_2_), channel_id=1, source_target_pairs={{0,1},{1,0},{2,3},{3,2},{4,5},{5,4},{6,7},{7,6},{8,9},{9,8},{10,11... | collective-permute-start | bytes 393224 | tf_op jit(solution)/shard_map/ppermute | solution.py:228
  24.3 7.5 %copy-start.5 = (bf16[4,128,128]{2,1,0:T(8,128)(2,1)}, bf16[4,128,128]{2,1,0:T(8,128)(2,1)S(1)}, u32[]{:S(2)}) copy-start(bf16[4,128,128]{2,1,0:T(8,128)(2,1)S(1)} %collective-permute-done.7.refs_6_) | copy-start | bytes 393220
  24.3 1.3 %collective-permute-start.6 = (bf16[4,128,128]{2,1,0:T(8,128)(2,1)S(1)}, bf16[4,128,128]{2,1,0:T(8,128)(2,1)S(1)}, u32[]{:S(2)}, u32[]{:S(2)}) collective-permute-start(bf16[4,128,128]{2,1,0:T(8,128)(2,1)S(1)} %collective-permute-done.5.refs_4_), channel_id=1, source_target_pairs={{0,1},{1,0},{2,3},{3,2},{4,5},{5,4},{6,7},{7,6},{8,9},{9,8},{10,11... | collective-permute-start | bytes 393224 | tf_op jit(solution)/shard_map/ppermute | solution.py:228
  24.4 7.4 %copy-start.6 = (bf16[4,128,128]{2,1,0:T(8,128)(2,1)}, bf16[4,128,128]{2,1,0:T(8,128)(2,1)S(1)}, u32[]{:S(2)}) copy-start(bf16[4,128,128]{2,1,0:T(8,128)(2,1)S(1)} %collective-permute-done.2.refs_1_) | copy-start | bytes 393220
  24.4 1.4 %collective-permute-start.8 = (bf16[4,128,128]{2,1,0:T(8,128)(2,1)S(1)}, bf16[4,128,128]{2,1,0:T(8,128)(2,1)S(1)}, u32[]{:S(2)}, u32[]{:S(2)}) collective-permute-start(bf16[4,128,128]{2,1,0:T(8,128)(2,1)S(1)} %collective-permute-done.7.refs_6_), channel_id=1, source_target_pairs={{0,1},{1,0},{2,3},{3,2},{4,5},{5,4},{6,7},{7,6},{8,9},{9,8},{10,11... | collective-permute-start | bytes 393224 | tf_op jit(solution)/shard_map/ppermute | solution.py:228
  24.8 7.0 %copy-start = (f32[85,512]{1,0:T(8,128)}, f32[85,512]{1,0:T(8,128)S(1)}, u32[]{:S(2)}) copy-start(f32[85,512]{1,0:T(8,128)S(1)} %collective-permute-done.before_ref.refs_8_) | copy-start | bytes 522244
  25.1 6.8 %copy-start.1 = (f32[85,512]{1,0:T(8,128)}, f32[85,512]{1,0:T(8,128)S(1)}, u32[]{:S(2)}) copy-start(f32[85,512]{1,0:T(8,128)S(1)} %collective-permute-done.1.after_ref.refs_9_) | copy-start | bytes 522244
  25.3 6.6 %copy-start.7 = (bf16[4,128,128]{2,1,0:T(8,128)(2,1)}, bf16[4,128,128]{2,1,0:T(8,128)(2,1)S(1)}, u32[]{:S(2)}) copy-start(bf16[4,128,128]{2,1,0:T(8,128)(2,1)S(1)} %collective-permute-done.4.refs_3_) | copy-start | bytes 393220
  25.7 6.2 %copy-start.8 = (bf16[4,128,128]{2,1,0:T(8,128)(2,1)}, bf16[4,128,128]{2,1,0:T(8,128)(2,1)S(1)}, u32[]{:S(2)}) copy-start(bf16[4,128,128]{2,1,0:T(8,128)(2,1)S(1)} %collective-permute-done.6.refs_5_) | copy-start | bytes 393220
  25.9 6.0 %copy-start.9 = (bf16[4,128,128]{2,1,0:T(8,128)(2,1)}, bf16[4,128,128]{2,1,0:T(8,128)(2,1)S(1)}, u32[]{:S(2)}) copy-start(bf16[4,128,128]{2,1,0:T(8,128)(2,1)S(1)} %collective-permute-done.8.refs_7_) | copy-start | bytes 393220
  36.1 26.5 %all-to-all-start.1 = ((bf16[16,64,640]{2,1,0:T(8,128)(2,1)}), bf16[16,64,640]{2,1,0:T(8,128)(2,1)S(1)}, u32[]{:S(2)}, u32[]{:S(2)}) async-start(bf16[16,64,640]{2,1,0:T(8,128)(2,1)} %shard_map.89), calls=%async_computation.1 | async-start | bytes 2621440 | tf_op jit(solution)/shard_map/all_to_all | solution.py:305

commit v3 on v2

--- a/solution.py
+++ b/solution.py
@@ -52,10 +52,15 @@
 
 
 def lane_rows(ref):
-    table = ref[...].astype(f32).reshape(K * TILES, NT)
+    table = ref[...].reshape(K * TILES, NT)
     lane = lax.broadcasted_iota(jnp.int32, (NT, ROWS), 1)
     pick = (lane // TILES == lax.broadcasted_iota(jnp.int32, (NT, ROWS), 0)).astype(f32)
-    spread = jnp.dot(table, pick, precision=lax.Precision.HIGHEST, preferred_element_type=f32)
+    if table.dtype == jnp.int32:
+        table = jnp.concatenate([table >> 4, table & 15], axis=0).astype(f32).astype(bf16)
+        spread = jnp.dot(table, pick.astype(bf16), preferred_element_type=f32)
+        spread = 16.0 * spread[: K * TILES] + spread[K * TILES :]
+    else:
+        spread = jnp.dot(table, pick, precision=lax.Precision.HIGHEST, preferred_element_type=f32)
     spread = spread.reshape(K, TILES, ROWS)
     sub = lax.broadcasted_iota(jnp.int32, (K, TILES, ROWS), 1)
     col = lax.broadcasted_iota(jnp.int32, (K, TILES, ROWS), 2)
@@ -177,23 +182,35 @@
         store.wait()
 
 
-def edges_kernel(cells_ref, dissipation_ref, first_ref, last_ref):
+def edges_kernel(cells_hbm, dissipation_ref, inner_ref, outer_ref, cells_ref, sem):
+    lanes = [pl.ds(i * 128, 128) for i in range(NP // 128)]
+    loads = [pltpu.make_async_copy(cells_hbm.at[:, l], cells_ref.at[i], sem.at[i]) for i, l in enumerate(lanes)]
+    for load in loads:
+        load.start()
+    core = lax.axis_index("core")
     count = NT * F
-    first_ref[...] = cells_ref[pl.ds(0, count, stride=LAYERS), :] * dissipation_ref[0:1, :]
-    last_ref[...] = cells_ref[pl.ds(LAYERS - 1, count, stride=LAYERS), :] * dissipation_ref[LAYERS - 1 :, :]
-
-
-def cells_kernel(cells_ref, jac_ref, dissipation_ref, before_ref, after_ref, out_ref):
+    for i, l in enumerate(lanes):
+        loads[i].wait()
+        first = cells_ref[i, pl.ds(0, count, stride=LAYERS), :] * dissipation_ref[0:1, l]
+        last = cells_ref[i, pl.ds(LAYERS - 1, count, stride=LAYERS), :] * dissipation_ref[LAYERS - 1 :, l]
+        inner_ref[:, l] = jnp.where(core == 0, last, first)
+        outer_ref[:, l] = jnp.where(core == 0, first, last)
+
+
+def cells_kernel(cells_ref, jac_ref, dissipation_ref, inner_ref, outer_ref, out_ref):
     dissipation = dissipation_ref[...]
     layer = lax.broadcasted_iota(jnp.int32, dissipation.shape, 0)
+    core = lax.axis_index("core")
+    before = jnp.where(core == 0, outer_ref[...], inner_ref[...])
+    after = jnp.where(core == 0, inner_ref[...], outer_ref[...])
     for g in range(F):
         values = [cells_ref[t, g] for t in range(NT)]
         total = time_sum(values)
         for t in range(NT):
             field = dissipation * values[t]
             at = t * F + g
-            lower = jnp.where(layer == 0, before_ref[at : at + 1, :], pltpu.roll(field, 1, 0))
-            upper = jnp.where(layer == LAYERS - 1, after_ref[at : at + 1, :], pltpu.roll(field, LAYERS - 1, 0))
+            lower = jnp.where(layer == 0, before[at : at + 1], pltpu.roll(field, 1, 0))
+            upper = jnp.where(layer == LAYERS - 1, after[at : at + 1], pltpu.roll(field, LAYERS - 1, 0))
             out_ref[t, g] = total[t] - (upper - 2.0 * field + lower)
     for t in range(NT):
         field = [cells_ref[t, f] for f in range(F)]
@@ -265,20 +282,17 @@
 
     edge = shape((NT * F, NP), f32)
     lanes = 128
-    first, last = call(
+    inner, outer = call(
         edges_kernel,
         (edge, edge),
         in_hbm(cells.reshape(NT * F * LAYERS, NP), dissipation),
-        grid=(NP // lanes,),
-        in_specs=[
-            pl.BlockSpec((NT * F * LAYERS, lanes), lambda i: (0, i)),
-            pl.BlockSpec((LAYERS, lanes), lambda i: (0, i)),
-        ],
-        out_specs=[pl.BlockSpec((NT * F, lanes), lambda i: (0, i))] * 2,
-    )
-    size = lax.axis_size(RADIAL)
-    before = lax.ppermute(last, RADIAL, [(i, i + 1) for i in range(size - 1)])
-    after = lax.ppermute(first, RADIAL, [(i + 1, i) for i in range(size - 1)])
+        in_specs=[hbm, vmem],
+        out_specs=[vmem, vmem],
+        scratch_shapes=[pltpu.VMEM((NP // lanes, NT * F * LAYERS, lanes), f32), dma((NP // lanes,))],
+    )
+    joints = [(i, i + 1) for i in range(1, lax.axis_size(RADIAL) - 1, 2)]
+    inner = shift(inner, "core", 1)
+    outer = lax.ppermute(outer, RADIAL, joints + [(j, i) for i, j in joints])
 
     weights, time_faces = call(
         weights_kernel,
@@ -287,11 +301,11 @@
         2 * ROWS * ROWS * SLOTS,
     )
 
-    before, after = in_hbm(before, after)
+    inner, outer = in_hbm(inner, outer)
     products = call(
         maps_kernel,
         pltpu.HBM((PEERS, SLOTS // PEERS, WIDTH), bf16),
-        (in_vmem(arrived), *in_hbm(*pieces), before, after),
+        (in_vmem(arrived), *in_hbm(*pieces), inner, outer),
         2 * SLOTS * F * 8 * FACE * FACE,
         in_specs=[vmem] + [hbm] * 10,
         out_specs=hbm,
@@ -307,7 +321,7 @@
     cell_gradient = call(
         cells_kernel,
         pltpu.HBM(cells.shape, f32),
-        in_hbm(cells, jac, dissipation, before, after),
+        in_hbm(cells, jac, dissipation, inner, outer),
         24 * NT * F * LAYERS * NP,
         grid=(NP // lanes,),
         in_specs=[

time: 66.7 us -> 66.1 us (level)
  the two profiles are of different devices: /device:TPU:0 before, /device:TPU:96 now
where the time goes in v3:
time: 66.1 us; the launch traced here: 65.6 us
  waiting for transfers between devices  23.4 us (35%)
  Pallas kernels  22.1 us (33%)
  starting transfers between devices  19.2 us (29%)
  between operations  0.79 us (1%)
    pallas_call x6, Pallas kernels, call(): pl.pallas_call(kernel, out_shape=outs, compiler_params=pltpu.CompilerPara...  22.1 us
    all_to_all x1, waiting for transfers between devices, body(): returned = lax.all_to_all(products, SPREAD, 0, 0, tiled=True)  13.1 us
    all_to_all x1, waiting for transfers between devices, body(): lax.all_to_all(outgoing.reshape(PEERS, SLOTS // PEERS, WIDTH), SPREAD, 0,...  7.97 us
    all_to_all x1, starting transfers between devices, body(): lax.all_to_all(outgoing.reshape(PEERS, SLOTS // PEERS, WIDTH), SPREAD, 0,...  7.19 us
    ppermute x8, starting transfers between devices, shift(): lax.ppermute(value, axis, [(i, (i + step) % size) for i in range(size)])  5.93 us
    all_to_all x1, starting transfers between devices, body(): returned = lax.all_to_all(products, SPREAD, 0, 0, tiled=True)  3.71 us
    ppermute x1, starting transfers between devices, body(): outer = lax.ppermute(outer, RADIAL, joints + [(j, i) for i, j in joints])  2.4 us
    ppermute x8, waiting for transfers between devices, shift(): lax.ppermute(value, axis, [(i, (i + step) % size) for i in range(size)])  1.41 us
  transfers between devices with their start and end apart: 11, of which 5 were waited for; matrix products, arithmetic and copies ran while one was open for 0% of the time, Pallas kernels for 17%

profile of v3, /device:TPU:96, one launch (start us, length us, event | category | flops | bytes accessed | tf_op | source)
XLA Modules:
  0.0 65.6 jit_solution(12918030988238171085)
XLA Ops:
  0.6 3.1 %shard_map.88 = bf16[1024,640]{1,0:T(8,128)(2,1)} custom-call(f32[17,5,16,128]{3,2,1,0:T(8,128)} %bitcast.24, s32[3,16,17]{2,1,0:T(8,128)} %bitcast.29), custom_call_target="tpu_custom_call" | custom-call | flops 713031680 | bytes 2010304 | tf_op jit(solution)/shard_map/pallas_call | solution.py:234
  3.7 0.0 copy-start.2
  3.7 7.2 %all-to-all-start = ((bf16[16,64,640]{2,1,0:T(8,128)(2,1)}), bf16[16,64,640]{2,1,0:T(8,128)(2,1)S(1)}, u32[]{:S(2)}, u32[]{:S(2)}) async-start(bf16[16,64,640]{2,1,0:T(8,128)(2,1)} %bitcast.23), calls=%async_computation | async-start | bytes 2621440 | tf_op jit(solution)/shard_map/all_to_all | solution.py:276
  10.9 0.1 collective-permute-start.3
  11.0 2.0 %collective-permute-start.5 = (bf16[4,128,128]{2,1,0:T(8,128)(2,1)S(1)}, bf16[4,128,128]{2,1,0:T(8,128)(2,1)S(1)}, u32[]{:S(2)}, u32[]{:S(2)}) collective-permute-start(bf16[4,128,128]{2,1,0:T(8,128)(2,1)S(1)} %copy-done.2), channel_id=1, source_target_pairs={{0,6},{2,0},{4,2},{6,4},{1,7},{3,1},{5,3},{7,5},{8,14},{10,8},{12,... | collective-permute-start | bytes 393224 | tf_op jit(solution)/shard_map/ppermute | solution.py:245
  13.0 0.6 collective-permute-start.7
  13.6 0.0 collective-permute-start.2
  13.6 2.1 %shard_map.86 = (f32[85,512]{1,0:T(8,128)S(1)}, f32[85,512]{1,0:T(8,128)S(1)}) custom-call(f32[680,512]{1,0:T(8,128)} %bitcast.19, f32[8,512]{1,0:T(8,128)} %bitcast.27), custom_call_target="tpu_custom_call" | custom-call | bytes 1757184 | tf_op jit(solution)/shard_map/pallas_call | solution.py:234
  15.7 0.6 collective-permute-start
  16.2 0.7 %collective-permute-done.3.refs_2_ = bf16[4,128,128]{2,1,0:T(8,128)(2,1)S(1)} collective-permute-done((bf16[4,128,128]{2,1,0:T(8,128)(2,1)S(1)}, bf16[4,128,128]{2,1,0:T(8,128)(2,1)S(1)}, u32[]{:S(2)}, u32[]{:S(2)}) %collective-permute-start.3) | collective-permute-done | bytes 131104 | tf_op jit(solution)/shard_map/ppermute | solution.py:245
  17.0 2.4 %collective-permute-start.1 = (f32[85,512]{1,0:T(8,128)S(1)}, f32[85,512]{1,0:T(8,128)S(1)}, u32[]{:S(2)}, u32[]{:S(2)}) collective-permute-start(f32[85,512]{1,0:T(8,128)S(1)} %get-tuple-element.7), channel_id=1, source_target_pairs={{1,2},{3,4},{5,6},{7,8},{9,10},{11,12},{13,14},{15,16},{17,18},{19... | collective-permute-start | bytes 522248 | tf_op jit(solution)/shard_map/ppermute | solution.py:295
  19.4 0.7 %collective-permute-done.5.refs_4_ = bf16[4,128,128]{2,1,0:T(8,128)(2,1)S(1)} collective-permute-done((bf16[4,128,128]{2,1,0:T(8,128)(2,1)S(1)}, bf16[4,128,128]{2,1,0:T(8,128)(2,1)S(1)}, u32[]{:S(2)}, u32[]{:S(2)}) %collective-permute-start.5) | collective-permute-done | bytes 131104 | tf_op jit(solution)/shard_map/ppermute | solution.py:245
  20.1 2.2 %collective-permute-start.4 = (bf16[4,128,128]{2,1,0:T(8,128)(2,1)S(1)}, bf16[4,128,128]{2,1,0:T(8,128)(2,1)S(1)}, u32[]{:S(2)}, u32[]{:S(2)}) collective-permute-start(bf16[4,128,128]{2,1,0:T(8,128)(2,1)S(1)} %collective-permute-done.3.refs_2_), channel_id=1, source_target_pairs={{0,1},{1,0},{2,3},{3,2},{4,5},{5,4},{6,7},{7,6},{8,9},{9,8},{10,11... | collective-permute-start | bytes 393224 | tf_op jit(solution)/shard_map/ppermute | solution.py:245
  22.2 0.0 collective-permute-done.7.refs_6_
  22.3 0.1 collective-permute-start.6
  22.4 0.0 collective-permute-done.2.refs_1_
  22.4 0.4 collective-permute-start.8
  22.8 0.0 collective-permute-done.inner_ref.refs_8_
  22.8 1.0 %collective-permute-done.1.outer_ref.refs_9_ = f32[85,512]{1,0:T(8,128)S(1)} collective-permute-done((f32[85,512]{1,0:T(8,128)S(1)}, f32[85,512]{1,0:T(8,128)S(1)}, u32[]{:S(2)}, u32[]{:S(2)}) %collective-permute-start.1) | collective-permute-done | bytes 174112 | tf_op jit(solution)/shard_map/ppermute | solution.py:295
  23.8 0.0 collective-permute-done.4.refs_3_
  23.8 0.0 collective-permute-done.6.refs_5_
  23.8 0.0 collective-permute-done.8.refs_7_
  23.8 8.0 %all-to-all-done.rows_ref = bf16[16,64,640]{2,1,0:T(8,128)(2,1)S(1)} async-done(((bf16[16,64,640]{2,1,0:T(8,128)(2,1)}), bf16[16,64,640]{2,1,0:T(8,128)(2,1)S(1)}, u32[]{:S(2)}, u32[]{:S(2)}) %all-to-all-start) | async-done | bytes 1310752 | tf_op jit(solution)/shard_map/all_to_all | solution.py:276
  31.8 0.0 copy-done.6
  31.8 0.0 copy-done
  31.8 0.0 copy-done.1
  31.9 4.1 %shard_map.89 = bf16[16,64,640]{2,1,0:T(8,128)(2,1)} custom-call(bf16[16,64,640]{2,1,0:T(8,128)(2,1)S(1)} %all-to-all-done.rows_ref, bf16[4,128,128]{2,1,0:T(8,128)(2,1)} %refs_0_.1, bf16[4,128,128]{2,1,0:T(8,128)(2,1)} %copy-done.6, bf16[4,128,128]{2,1,0:T(8,128)(2,1)} %copy-done.3, bf16[4,128,128]{2,1,0:T(8,128)(2,1)} %copy-done.7, ...), custom_call_target="tpu_custom_call" | custom-call | flops 1342177280 | bytes 4018176 | tf_op jit(solution)/shard_map/pallas_call | solution.py:234
  36.0 3.7 %all-to-all-start.1 = ((bf16[16,64,640]{2,1,0:T(8,128)(2,1)}), bf16[16,64,640]{2,1,0:T(8,128)(2,1)S(1)}, u32[]{:S(2)}, u32[]{:S(2)}) async-start(bf16[16,64,640]{2,1,0:T(8,128)(2,1)} %shard_map.89), calls=%async_computation.1 | async-start | bytes 2621440 | tf_op jit(solution)/shard_map/all_to_all | solution.py:319
  39.7 3.9 %shard_map.90 = (bf16[2,272,1024]{2,1,0:T(8,128)(2,1)}, f32[17,5,16,128]{3,2,1,0:T(8,128)}) custom-call(f32[17,5,16,128]{3,2,1,0:T(8,128)} %bitcast.25, s32[3,16,17]{2,1,0:T(8,128)} %bitcast.30, f32[3,16,17]{2,1,0:T(8,128)} %bitcast.31), custom_call_target="tpu_custom_call" | custom-call | flops 151519232 | bytes 2513280 | tf_op jit(solution)/shard_map/pallas_call | solution.py:234
  43.6 5.2 %shard_map.87 = f32[17,5,8,512]{3,2,1,0:T(8,128)} custom-call(f32[17,5,8,512]{3,2,1,0:T(8,128)} %bitcast.20, bf16[17,5,5,8,512]{4,3,2,1,0:T(8,128)(2,1)} %bitcast.21, f32[8,512]{1,0:T(8,128)} %bitcast.28, f32[85,512]{1,0:T(8,128)} %copy-done, f32[85,512]{1,0:T(8,128)} %copy-done.1), custom_call_target="tpu_custom_call" | custom-call | flops 8355840 | bytes 6631424 | tf_op jit(solution)/shard_map/pallas_call | solution.py:234
  48.8 13.1 %all-to-all-done.1 = bf16[16,64,640]{2,1,0:T(8,128)(2,1)S(1)} async-done(((bf16[16,64,640]{2,1,0:T(8,128)(2,1)}), bf16[16,64,640]{2,1,0:T(8,128)(2,1)S(1)}, u32[]{:S(2)}, u32[]{:S(2)}) %all-to-all-start.1) | async-done | bytes 1310752 | tf_op jit(solution)/shard_map/all_to_all | solution.py:319
  61.9 3.7 %shard_map.91 = f32[17,5,16,128]{3,2,1,0:T(8,128)} custom-call(bf16[1024,640]{1,0:T(8,128)(2,1)S(1)} %bitcast.18, bf16[2,272,1024]{2,1,0:T(8,128)(2,1)} %get-tuple-element.8.weight_hbm, f32[17,5,16,128]{3,2,1,0:T(8,128)} %get-tuple-element.9.time_hbm), custom_call_target="tpu_custom_call" | custom-call | flops 713031680 | bytes 3817472 | tf_op jit(solution)/shard_map/pallas_call | solution.py:234
  (16 shorter events, 0.0 us)
Async XLA Ops:
  3.7 7.2 %copy-start.2 = (bf16[4,128,128]{2,1,0:T(8,128)(2,1)S(1)}, bf16[4,128,128]{2,1,0:T(8,128)(2,1)}, u32[]{:S(2)}) copy-start(bf16[4,128,128]{2,1,0:T(8,128)(2,1)} %refs_0_.1) | copy-start | bytes 393220
  3.7 28.1 %all-to-all-start = ((bf16[16,64,640]{2,1,0:T(8,128)(2,1)}), bf16[16,64,640]{2,1,0:T(8,128)(2,1)S(1)}, u32[]{:S(2)}, u32[]{:S(2)}) async-start(bf16[16,64,640]{2,1,0:T(8,128)(2,1)} %bitcast.23), calls=%async_computation | async-start | bytes 2621440 | tf_op jit(solution)/shard_map/all_to_all | solution.py:276
  10.9 6.1 %collective-permute-start.3 = (bf16[4,128,128]{2,1,0:T(8,128)(2,1)S(1)}, bf16[4,128,128]{2,1,0:T(8,128)(2,1)S(1)}, u32[]{:S(2)}, u32[]{:S(2)}) collective-permute-start(bf16[4,128,128]{2,1,0:T(8,128)(2,1)S(1)} %copy-done.2), channel_id=1, source_target_pairs={{0,2},{2,4},{4,6},{6,0},{1,3},{3,5},{5,7},{7,1},{8,10},{10,12},{12... | collective-permute-start | bytes 393224 | tf_op jit(solution)/shard_map/ppermute | solution.py:245
  11.0 9.1 %collective-permute-start.5 = (bf16[4,128,128]{2,1,0:T(8,128)(2,1)S(1)}, bf16[4,128,128]{2,1,0:T(8,128)(2,1)S(1)}, u32[]{:S(2)}, u32[]{:S(2)}) collective-permute-start(bf16[4,128,128]{2,1,0:T(8,128)(2,1)S(1)} %copy-done.2), channel_id=1, source_target_pairs={{0,6},{2,0},{4,2},{6,4},{1,7},{3,1},{5,3},{7,5},{8,14},{10,8},{12,... | collective-permute-start | bytes 393224 | tf_op jit(solution)/shard_map/ppermute | solution.py:245
  13.0 9.2 %collective-permute-start.7 = (bf16[4,128,128]{2,1,0:T(8,128)(2,1)S(1)}, bf16[4,128,128]{2,1,0:T(8,128)(2,1)S(1)}, u32[]{:S(2)}, u32[]{:S(2)}) collective-permute-start(bf16[4,128,128]{2,1,0:T(8,128)(2,1)S(1)} %copy-done.2), channel_id=1, source_target_pairs={{0,4},{2,6},{4,0},{6,2},{1,5},{3,7},{5,1},{7,3},{8,12},{10,14},{12... | collective-permute-start | bytes 393224 | tf_op jit(solution)/shard_map/ppermute | solution.py:245
  13.6 8.8 %collective-permute-start.2 = (bf16[4,128,128]{2,1,0:T(8,128)(2,1)S(1)}, bf16[4,128,128]{2,1,0:T(8,128)(2,1)S(1)}, u32[]{:S(2)}, u32[]{:S(2)}) collective-permute-start(bf16[4,128,128]{2,1,0:T(8,128)(2,1)S(1)} %copy-done.2), channel_id=1, source_target_pairs={{0,1},{1,0},{2,3},{3,2},{4,5},{5,4},{6,7},{7,6},{8,9},{9,8},{10,11... | collective-permute-start | bytes 393224 | tf_op jit(solution)/shard_map/ppermute | solution.py:245
  15.7 7.1 %collective-permute-start = (f32[85,512]{1,0:T(8,128)S(1)}, f32[85,512]{1,0:T(8,128)S(1)}, u32[]{:S(2)}, u32[]{:S(2)}) collective-permute-start(f32[85,512]{1,0:T(8,128)S(1)} %get-tuple-element.6), channel_id=1, source_target_pairs={{0,1},{1,0},{2,3},{3,2},{4,5},{5,4},{6,7},{7,6},{8,9},{9,8},{10,11... | collective-permute-start | bytes 522248 | tf_op jit(solution)/shard_map/ppermute | solution.py:245
  17.0 14.8 %copy-start.3 = (bf16[4,128,128]{2,1,0:T(8,128)(2,1)}, bf16[4,128,128]{2,1,0:T(8,128)(2,1)S(1)}, u32[]{:S(2)}) copy-start(bf16[4,128,128]{2,1,0:T(8,128)(2,1)S(1)} %collective-permute-done.3.refs_2_) | copy-start | bytes 393220
  17.0 6.8 %collective-permute-start.1 = (f32[85,512]{1,0:T(8,128)S(1)}, f32[85,512]{1,0:T(8,128)S(1)}, u32[]{:S(2)}, u32[]{:S(2)}) collective-permute-start(f32[85,512]{1,0:T(8,128)S(1)} %get-tuple-element.7), channel_id=1, source_target_pairs={{1,2},{3,4},{5,6},{7,8},{9,10},{11,12},{13,14},{15,16},{17,18},{19... | collective-permute-start | bytes 522248 | tf_op jit(solution)/shard_map/ppermute | solution.py:295
  20.1 11.7 %copy-start.4 = (bf16[4,128,128]{2,1,0:T(8,128)(2,1)}, bf16[4,128,128]{2,1,0:T(8,128)(2,1)S(1)}, u32[]{:S(2)}) copy-start(bf16[4,128,128]{2,1,0:T(8,128)(2,1)S(1)} %collective-permute-done.5.refs_4_) | copy-start | bytes 393220
  20.1 3.7 %collective-permute-start.4 = (bf16[4,128,128]{2,1,0:T(8,128)(2,1)S(1)}, bf16[4,128,128]{2,1,0:T(8,128)(2,1)S(1)}, u32[]{:S(2)}, u32[]{:S(2)}) collective-permute-start(bf16[4,128,128]{2,1,0:T(8,128)(2,1)S(1)} %collective-permute-done.3.refs_2_), channel_id=1, source_target_pairs={{0,1},{1,0},{2,3},{3,2},{4,5},{5,4},{6,7},{7,6},{8,9},{9,8},{10,11... | collective-permute-start | bytes 393224 | tf_op jit(solution)/shard_map/ppermute | solution.py:245
  22.3 9.6 %copy-start.5 = (bf16[4,128,128]{2,1,0:T(8,128)(2,1)}, bf16[4,128,128]{2,1,0:T(8,128)(2,1)S(1)}, u32[]{:S(2)}) copy-start(bf16[4,128,128]{2,1,0:T(8,128)(2,1)S(1)} %collective-permute-done.7.refs_6_) | copy-start | bytes 393220
  22.3 1.5 %collective-permute-start.6 = (bf16[4,128,128]{2,1,0:T(8,128)(2,1)S(1)}, bf16[4,128,128]{2,1,0:T(8,128)(2,1)S(1)}, u32[]{:S(2)}, u32[]{:S(2)}) collective-permute-start(bf16[4,128,128]{2,1,0:T(8,128)(2,1)S(1)} %collective-permute-done.5.refs_4_), channel_id=1, source_target_pairs={{0,1},{1,0},{2,3},{3,2},{4,5},{5,4},{6,7},{7,6},{8,9},{9,8},{10,11... | collective-permute-start | bytes 393224 | tf_op jit(solution)/shard_map/ppermute | solution.py:245
  22.4 9.4 %copy-start.6 = (bf16[4,128,128]{2,1,0:T(8,128)(2,1)}, bf16[4,128,128]{2,1,0:T(8,128)(2,1)S(1)}, u32[]{:S(2)}) copy-start(bf16[4,128,128]{2,1,0:T(8,128)(2,1)S(1)} %collective-permute-done.2.refs_1_) | copy-start | bytes 393220
  22.4 1.4 %collective-permute-start.8 = (bf16[4,128,128]{2,1,0:T(8,128)(2,1)S(1)}, bf16[4,128,128]{2,1,0:T(8,128)(2,1)S(1)}, u32[]{:S(2)}, u32[]{:S(2)}) collective-permute-start(bf16[4,128,128]{2,1,0:T(8,128)(2,1)S(1)} %collective-permute-done.7.refs_6_), channel_id=1, source_target_pairs={{0,1},{1,0},{2,3},{3,2},{4,5},{5,4},{6,7},{7,6},{8,9},{9,8},{10,11... | collective-permute-start | bytes 393224 | tf_op jit(solution)/shard_map/ppermute | solution.py:245
  22.8 9.0 %copy-start = (f32[85,512]{1,0:T(8,128)}, f32[85,512]{1,0:T(8,128)S(1)}, u32[]{:S(2)}) copy-start(f32[85,512]{1,0:T(8,128)S(1)} %collective-permute-done.inner_ref.refs_8_) | copy-start | bytes 522244
  23.8 8.0 %copy-start.1 = (f32[85,512]{1,0:T(8,128)}, f32[85,512]{1,0:T(8,128)S(1)}, u32[]{:S(2)}) copy-start(f32[85,512]{1,0:T(8,128)S(1)} %collective-permute-done.1.outer_ref.refs_9_) | copy-start | bytes 522244
  23.8 8.0 %copy-start.7 = (bf16[4,128,128]{2,1,0:T(8,128)(2,1)}, bf16[4,128,128]{2,1,0:T(8,128)(2,1)S(1)}, u32[]{:S(2)}) copy-start(bf16[4,128,128]{2,1,0:T(8,128)(2,1)S(1)} %collective-permute-done.4.refs_3_) | copy-start | bytes 393220
  23.8 8.1 %copy-start.8 = (bf16[4,128,128]{2,1,0:T(8,128)(2,1)}, bf16[4,128,128]{2,1,0:T(8,128)(2,1)S(1)}, u32[]{:S(2)}) copy-start(bf16[4,128,128]{2,1,0:T(8,128)(2,1)S(1)} %collective-permute-done.6.refs_5_) | copy-start | bytes 393220
  23.8 8.0 %copy-start.9 = (bf16[4,128,128]{2,1,0:T(8,128)(2,1)}, bf16[4,128,128]{2,1,0:T(8,128)(2,1)S(1)}, u32[]{:S(2)}) copy-start(bf16[4,128,128]{2,1,0:T(8,128)(2,1)S(1)} %collective-permute-done.8.refs_7_) | copy-start | bytes 393220
  36.0 25.9 %all-to-all-start.1 = ((bf16[16,64,640]{2,1,0:T(8,128)(2,1)}), bf16[16,64,640]{2,1,0:T(8,128)(2,1)S(1)}, u32[]{:S(2)}, u32[]{:S(2)}) async-start(bf16[16,64,640]{2,1,0:T(8,128)(2,1)} %shard_map.89), calls=%async_computation.1 | async-start | bytes 2621440 | tf_op jit(solution)/shard_map/all_to_all | solution.py:319

commit v4 on v3

--- a/solution.py
+++ b/solution.py
@@ -201,8 +201,10 @@
     dissipation = dissipation_ref[...]
     layer = lax.broadcasted_iota(jnp.int32, dissipation.shape, 0)
     core = lax.axis_index("core")
-    before = jnp.where(core == 0, outer_ref[...], inner_ref[...])
-    after = jnp.where(core == 0, inner_ref[...], outer_ref[...])
+    place = lax.axis_index("y") * 8 + lax.axis_index("z") * 2 + core
+    outer = jnp.where((place == 0) | (place == 31), 0.0, outer_ref[...])
+    before = jnp.where(core == 0, outer, inner_ref[...])
+    after = jnp.where(core == 0, inner_ref[...], outer)
     for g in range(F):
         values = [cells_ref[t, g] for t in range(NT)]
         total = time_sum(values)
@@ -290,7 +292,8 @@
         out_specs=[vmem, vmem],
         scratch_shapes=[pltpu.VMEM((NP // lanes, NT * F * LAYERS, lanes), f32), dma((NP // lanes,))],
     )
-    joints = [(i, i + 1) for i in range(1, lax.axis_size(RADIAL) - 1, 2)]
+    size = lax.axis_size(RADIAL)
+    joints = [(i, (i + 1) % size) for i in range(1, size, 2)]
     inner = shift(inner, "core", 1)
     outer = lax.ppermute(outer, RADIAL, joints + [(j, i) for i, j in joints])
 

time: 66.1 us -> 65.3 us (0.988)
  starting transfers between devices: 19.2 us -> 15.4 us
  waiting for transfers between devices: 23.4 us -> 26.5 us
    ppermute x8, starting transfers between devices: 5.93 us -> 3.93 us  [shift(): lax.ppermute(value, axis, [(i, (i + step) % size) for i in range(size)])]
    all_to_all x1, waiting for transfers between devices: 7.97 us -> 9.85 us  [body(): lax.all_to_all(outgoing.reshape(PEERS, SLOTS // PEERS, WIDTH), SPREAD, 0,...]
    ppermute x8, waiting for transfers between devices: 1.41 us -> 3.25 us  [shift(): lax.ppermute(value, axis, [(i, (i + step) % size) for i in range(size)])]
    ppermute x1, starting transfers between devices: 2.4 us -> 0.58 us  [body(): outer = lax.ppermute(outer, RADIAL, joints + [(j, i) for i, j in joints])]
    all_to_all x1, waiting for transfers between devices: 13.1 us -> 12.3 us  [body(): returned = lax.all_to_all(products, SPREAD, 0, 0, tiled=True)]
where the time goes in v4:
time: 65.3 us; the launch traced here: 64.8 us
  waiting for transfers between devices  26.5 us (41%)
  Pallas kernels  22 us (34%)
  starting transfers between devices  15.4 us (24%)
  between operations  0.78 us (1%)
    pallas_call x6, Pallas kernels, call(): pl.pallas_call(kernel, out_shape=outs, compiler_params=pltpu.CompilerPara...  22 us
    all_to_all x1, waiting for transfers between devices, body(): returned = lax.all_to_all(products, SPREAD, 0, 0, tiled=True)  12.3 us
    all_to_all x1, waiting for transfers between devices, body(): lax.all_to_all(outgoing.reshape(PEERS, SLOTS // PEERS, WIDTH), SPREAD, 0,...  9.85 us
    all_to_all x1, starting transfers between devices, body(): lax.all_to_all(outgoing.reshape(PEERS, SLOTS // PEERS, WIDTH), SPREAD, 0,...  7.19 us
    ppermute x8, starting transfers between devices, shift(): lax.ppermute(value, axis, [(i, (i + step) % size) for i in range(size)])  3.93 us
    all_to_all x1, starting transfers between devices, body(): returned = lax.all_to_all(products, SPREAD, 0, 0, tiled=True)  3.71 us
    ppermute x8, waiting for transfers between devices, shift(): lax.ppermute(value, axis, [(i, (i + step) % size) for i in range(size)])  3.25 us
  transfers between devices with their start and end apart: 11, of which 5 were waited for; matrix products, arithmetic and copies ran while one was open for 0% of the time, Pallas kernels for 17%

profile of v4, /device:TPU:96, one launch (start us, length us, event | category | flops | bytes accessed | tf_op | source)
XLA Modules:
  0.0 64.8 jit_solution(15557777992458434441)
XLA Ops:
  0.6 3.1 %shard_map.88 = bf16[1024,640]{1,0:T(8,128)(2,1)} custom-call(f32[17,5,16,128]{3,2,1,0:T(8,128)} %bitcast.24, s32[3,16,17]{2,1,0:T(8,128)} %bitcast.29), custom_call_target="tpu_custom_call" | custom-call | flops 713031680 | bytes 2010304 | tf_op jit(solution)/shard_map/pallas_call | solution.py:236
  3.7 0.0 copy-start.2
  3.7 7.2 %all-to-all-start = ((bf16[16,64,640]{2,1,0:T(8,128)(2,1)}), bf16[16,64,640]{2,1,0:T(8,128)(2,1)S(1)}, u32[]{:S(2)}, u32[]{:S(2)}) async-start(bf16[16,64,640]{2,1,0:T(8,128)(2,1)} %bitcast.23), calls=%async_computation | async-start | bytes 2621440 | tf_op jit(solution)/shard_map/all_to_all | solution.py:278
  10.9 0.0 copy-done.2
  10.9 0.1 collective-permute-start.3
  11.0 2.0 %collective-permute-start.5 = (bf16[4,128,128]{2,1,0:T(8,128)(2,1)S(1)}, bf16[4,128,128]{2,1,0:T(8,128)(2,1)S(1)}, u32[]{:S(2)}, u32[]{:S(2)}) collective-permute-start(bf16[4,128,128]{2,1,0:T(8,128)(2,1)S(1)} %copy-done.2), channel_id=1, source_target_pairs={{0,6},{2,0},{4,2},{6,4},{1,7},{3,1},{5,3},{7,5},{8,14},{10,8},{12,... | collective-permute-start | bytes 393224 | tf_op jit(solution)/shard_map/ppermute | solution.py:247
  13.0 0.6 collective-permute-start.7
  13.6 0.0 collective-permute-start.2
  13.6 2.1 %shard_map.86 = (f32[85,512]{1,0:T(8,128)S(1)}, f32[85,512]{1,0:T(8,128)S(1)}) custom-call(f32[680,512]{1,0:T(8,128)} %bitcast.19, f32[8,512]{1,0:T(8,128)} %bitcast.27), custom_call_target="tpu_custom_call" | custom-call | bytes 1757184 | tf_op jit(solution)/shard_map/pallas_call | solution.py:236
  15.7 0.6 collective-permute-start
  16.2 0.7 %collective-permute-done.3.refs_2_ = bf16[4,128,128]{2,1,0:T(8,128)(2,1)S(1)} collective-permute-done((bf16[4,128,128]{2,1,0:T(8,128)(2,1)S(1)}, bf16[4,128,128]{2,1,0:T(8,128)(2,1)S(1)}, u32[]{:S(2)}, u32[]{:S(2)}) %collective-permute-start.3) | collective-permute-done | bytes 131104 | tf_op jit(solution)/shard_map/ppermute | solution.py:247
  17.0 0.6 collective-permute-start.1
  17.6 2.5 %collective-permute-done.5.refs_4_ = bf16[4,128,128]{2,1,0:T(8,128)(2,1)S(1)} collective-permute-done((bf16[4,128,128]{2,1,0:T(8,128)(2,1)S(1)}, bf16[4,128,128]{2,1,0:T(8,128)(2,1)S(1)}, u32[]{:S(2)}, u32[]{:S(2)}) %collective-permute-start.5) | collective-permute-done | bytes 131104 | tf_op jit(solution)/shard_map/ppermute | solution.py:247
  20.1 0.2 collective-permute-start.4
  20.3 0.0 collective-permute-done.7.refs_6_
  20.3 0.3 collective-permute-start.6
  20.6 0.0 collective-permute-done.2.refs_1_
  20.6 0.2 collective-permute-start.8
  20.8 0.0 collective-permute-done.inner_ref.refs_8_
  20.8 1.1 %collective-permute-done.1.outer_ref.refs_9_ = f32[85,512]{1,0:T(8,128)S(1)} collective-permute-done((f32[85,512]{1,0:T(8,128)S(1)}, f32[85,512]{1,0:T(8,128)S(1)}, u32[]{:S(2)}, u32[]{:S(2)}) %collective-permute-start.1) | collective-permute-done | bytes 174112 | tf_op jit(solution)/shard_map/ppermute | solution.py:298
  21.9 0.0 collective-permute-done.4.refs_3_
  21.9 0.0 collective-permute-done.6.refs_5_
  21.9 0.0 collective-permute-done.8.refs_7_
  21.9 0.0 copy-start.9
  21.9 9.9 %all-to-all-done.rows_ref = bf16[16,64,640]{2,1,0:T(8,128)(2,1)S(1)} async-done(((bf16[16,64,640]{2,1,0:T(8,128)(2,1)}), bf16[16,64,640]{2,1,0:T(8,128)(2,1)S(1)}, u32[]{:S(2)}, u32[]{:S(2)}) %all-to-all-start) | async-done | bytes 1310752 | tf_op jit(solution)/shard_map/all_to_all | solution.py:278
  31.8 0.0 copy-done.5
  31.9 4.1 %shard_map.89 = bf16[16,64,640]{2,1,0:T(8,128)(2,1)} custom-call(bf16[16,64,640]{2,1,0:T(8,128)(2,1)S(1)} %all-to-all-done.rows_ref, bf16[4,128,128]{2,1,0:T(8,128)(2,1)} %refs_0_.1, bf16[4,128,128]{2,1,0:T(8,128)(2,1)} %copy-done.6, bf16[4,128,128]{2,1,0:T(8,128)(2,1)} %copy-done.3, bf16[4,128,128]{2,1,0:T(8,128)(2,1)} %copy-done.7, ...), custom_call_target="tpu_custom_call" | custom-call | flops 1342177280 | bytes 4018176 | tf_op jit(solution)/shard_map/pallas_call | solution.py:236
  36.0 3.7 %all-to-all-start.1 = ((bf16[16,64,640]{2,1,0:T(8,128)(2,1)}), bf16[16,64,640]{2,1,0:T(8,128)(2,1)S(1)}, u32[]{:S(2)}, u32[]{:S(2)}) async-start(bf16[16,64,640]{2,1,0:T(8,128)(2,1)} %shard_map.89), calls=%async_computation.1 | async-start | bytes 2621440 | tf_op jit(solution)/shard_map/all_to_all | solution.py:322
  39.7 3.9 %shard_map.90 = (bf16[2,272,1024]{2,1,0:T(8,128)(2,1)}, f32[17,5,16,128]{3,2,1,0:T(8,128)}) custom-call(f32[17,5,16,128]{3,2,1,0:T(8,128)} %bitcast.25, s32[3,16,17]{2,1,0:T(8,128)} %bitcast.30, f32[3,16,17]{2,1,0:T(8,128)} %bitcast.31), custom_call_target="tpu_custom_call" | custom-call | flops 151519232 | bytes 2513280 | tf_op jit(solution)/shard_map/pallas_call | solution.py:236
  43.6 5.2 %shard_map.87 = f32[17,5,8,512]{3,2,1,0:T(8,128)} custom-call(f32[17,5,8,512]{3,2,1,0:T(8,128)} %bitcast.20, bf16[17,5,5,8,512]{4,3,2,1,0:T(8,128)(2,1)} %bitcast.21, f32[8,512]{1,0:T(8,128)} %bitcast.28, f32[85,512]{1,0:T(8,128)} %copy-done, f32[85,512]{1,0:T(8,128)} %copy-done.1), custom_call_target="tpu_custom_call" | custom-call | flops 8355840 | bytes 6631424 | tf_op jit(solution)/shard_map/pallas_call | solution.py:236
  48.8 12.3 %all-to-all-done.1 = bf16[16,64,640]{2,1,0:T(8,128)(2,1)S(1)} async-done(((bf16[16,64,640]{2,1,0:T(8,128)(2,1)}), bf16[16,64,640]{2,1,0:T(8,128)(2,1)S(1)}, u32[]{:S(2)}, u32[]{:S(2)}) %all-to-all-start.1) | async-done | bytes 1310752 | tf_op jit(solution)/shard_map/all_to_all | solution.py:322
  61.1 3.7 %shard_map.91 = f32[17,5,16,128]{3,2,1,0:T(8,128)} custom-call(bf16[1024,640]{1,0:T(8,128)(2,1)S(1)} %bitcast.18, bf16[2,272,1024]{2,1,0:T(8,128)(2,1)} %get-tuple-element.8.weight_hbm, f32[17,5,16,128]{3,2,1,0:T(8,128)} %get-tuple-element.9.time_hbm), custom_call_target="tpu_custom_call" | custom-call | flops 713031680 | bytes 3817472 | tf_op jit(solution)/shard_map/pallas_call | solution.py:236
  (16 shorter events, 0.0 us)
Async XLA Ops:
  3.7 7.2 %copy-start.2 = (bf16[4,128,128]{2,1,0:T(8,128)(2,1)S(1)}, bf16[4,128,128]{2,1,0:T(8,128)(2,1)}, u32[]{:S(2)}) copy-start(bf16[4,128,128]{2,1,0:T(8,128)(2,1)} %refs_0_.1) | copy-start | bytes 393220
  3.7 28.1 %all-to-all-start = ((bf16[16,64,640]{2,1,0:T(8,128)(2,1)}), bf16[16,64,640]{2,1,0:T(8,128)(2,1)S(1)}, u32[]{:S(2)}, u32[]{:S(2)}) async-start(bf16[16,64,640]{2,1,0:T(8,128)(2,1)} %bitcast.23), calls=%async_computation | async-start | bytes 2621440 | tf_op jit(solution)/shard_map/all_to_all | solution.py:278
  10.9 6.1 %collective-permute-start.3 = (bf16[4,128,128]{2,1,0:T(8,128)(2,1)S(1)}, bf16[4,128,128]{2,1,0:T(8,128)(2,1)S(1)}, u32[]{:S(2)}, u32[]{:S(2)}) collective-permute-start(bf16[4,128,128]{2,1,0:T(8,128)(2,1)S(1)} %copy-done.2), channel_id=1, source_target_pairs={{0,2},{2,4},{4,6},{6,0},{1,3},{3,5},{5,7},{7,1},{8,10},{10,12},{12... | collective-permute-start | bytes 393224 | tf_op jit(solution)/shard_map/ppermute | solution.py:247
  11.0 9.1 %collective-permute-start.5 = (bf16[4,128,128]{2,1,0:T(8,128)(2,1)S(1)}, bf16[4,128,128]{2,1,0:T(8,128)(2,1)S(1)}, u32[]{:S(2)}, u32[]{:S(2)}) collective-permute-start(bf16[4,128,128]{2,1,0:T(8,128)(2,1)S(1)} %copy-done.2), channel_id=1, source_target_pairs={{0,6},{2,0},{4,2},{6,4},{1,7},{3,1},{5,3},{7,5},{8,14},{10,8},{12,... | collective-permute-start | bytes 393224 | tf_op jit(solution)/shard_map/ppermute | solution.py:247
  13.0 7.2 %collective-permute-start.7 = (bf16[4,128,128]{2,1,0:T(8,128)(2,1)S(1)}, bf16[4,128,128]{2,1,0:T(8,128)(2,1)S(1)}, u32[]{:S(2)}, u32[]{:S(2)}) collective-permute-start(bf16[4,128,128]{2,1,0:T(8,128)(2,1)S(1)} %copy-done.2), channel_id=1, source_target_pairs={{0,4},{2,6},{4,0},{6,2},{1,5},{3,7},{5,1},{7,3},{8,12},{10,14},{12... | collective-permute-start | bytes 393224 | tf_op jit(solution)/shard_map/ppermute | solution.py:247
  13.6 7.0 %collective-permute-start.2 = (bf16[4,128,128]{2,1,0:T(8,128)(2,1)S(1)}, bf16[4,128,128]{2,1,0:T(8,128)(2,1)S(1)}, u32[]{:S(2)}, u32[]{:S(2)}) collective-permute-start(bf16[4,128,128]{2,1,0:T(8,128)(2,1)S(1)} %copy-done.2), channel_id=1, source_target_pairs={{0,1},{1,0},{2,3},{3,2},{4,5},{5,4},{6,7},{7,6},{8,9},{9,8},{10,11... | collective-permute-start | bytes 393224 | tf_op jit(solution)/shard_map/ppermute | solution.py:247
  15.7 5.1 %collective-permute-start = (f32[85,512]{1,0:T(8,128)S(1)}, f32[85,512]{1,0:T(8,128)S(1)}, u32[]{:S(2)}, u32[]{:S(2)}) collective-permute-start(f32[85,512]{1,0:T(8,128)S(1)} %get-tuple-element.6), channel_id=1, source_target_pairs={{0,1},{1,0},{2,3},{3,2},{4,5},{5,4},{6,7},{7,6},{8,9},{9,8},{10,11... | collective-permute-start | bytes 522248 | tf_op jit(solution)/shard_map/ppermute | solution.py:247
  17.0 14.8 %copy-start.3 = (bf16[4,128,128]{2,1,0:T(8,128)(2,1)}, bf16[4,128,128]{2,1,0:T(8,128)(2,1)S(1)}, u32[]{:S(2)}) copy-start(bf16[4,128,128]{2,1,0:T(8,128)(2,1)S(1)} %collective-permute-done.3.refs_2_) | copy-start | bytes 393220
  17.0 4.9 %collective-permute-start.1 = (f32[85,512]{1,0:T(8,128)S(1)}, f32[85,512]{1,0:T(8,128)S(1)}, u32[]{:S(2)}, u32[]{:S(2)}) collective-permute-start(f32[85,512]{1,0:T(8,128)S(1)} %get-tuple-element.7), channel_id=1, source_target_pairs={{1,2},{3,4},{5,6},{7,8},{9,10},{11,12},{13,14},{15,16},{17,18},{19... | collective-permute-start | bytes 522248 | tf_op jit(solution)/shard_map/ppermute | solution.py:298
  20.1 11.7 %copy-start.4 = (bf16[4,128,128]{2,1,0:T(8,128)(2,1)}, bf16[4,128,128]{2,1,0:T(8,128)(2,1)S(1)}, u32[]{:S(2)}) copy-start(bf16[4,128,128]{2,1,0:T(8,128)(2,1)S(1)} %collective-permute-done.5.refs_4_) | copy-start | bytes 393220
  20.1 1.8 %collective-permute-start.4 = (bf16[4,128,128]{2,1,0:T(8,128)(2,1)S(1)}, bf16[4,128,128]{2,1,0:T(8,128)(2,1)S(1)}, u32[]{:S(2)}, u32[]{:S(2)}) collective-permute-start(bf16[4,128,128]{2,1,0:T(8,128)(2,1)S(1)} %collective-permute-done.3.refs_2_), channel_id=1, source_target_pairs={{0,1},{1,0},{2,3},{3,2},{4,5},{5,4},{6,7},{7,6},{8,9},{9,8},{10,11... | collective-permute-start | bytes 393224 | tf_op jit(solution)/shard_map/ppermute | solution.py:247
  20.3 11.6 %copy-start.5 = (bf16[4,128,128]{2,1,0:T(8,128)(2,1)}, bf16[4,128,128]{2,1,0:T(8,128)(2,1)S(1)}, u32[]{:S(2)}) copy-start(bf16[4,128,128]{2,1,0:T(8,128)(2,1)S(1)} %collective-permute-done.7.refs_6_) | copy-start | bytes 393220
  20.3 1.7 %collective-permute-start.6 = (bf16[4,128,128]{2,1,0:T(8,128)(2,1)S(1)}, bf16[4,128,128]{2,1,0:T(8,128)(2,1)S(1)}, u32[]{:S(2)}, u32[]{:S(2)}) collective-permute-start(bf16[4,128,128]{2,1,0:T(8,128)(2,1)S(1)} %collective-permute-done.5.refs_4_), channel_id=1, source_target_pairs={{0,1},{1,0},{2,3},{3,2},{4,5},{5,4},{6,7},{7,6},{8,9},{9,8},{10,11... | collective-permute-start | bytes 393224 | tf_op jit(solution)/shard_map/ppermute | solution.py:247
  20.6 11.2 %copy-start.6 = (bf16[4,128,128]{2,1,0:T(8,128)(2,1)}, bf16[4,128,128]{2,1,0:T(8,128)(2,1)S(1)}, u32[]{:S(2)}) copy-start(bf16[4,128,128]{2,1,0:T(8,128)(2,1)S(1)} %collective-permute-done.2.refs_1_) | copy-start | bytes 393220
  20.6 1.3 %collective-permute-start.8 = (bf16[4,128,128]{2,1,0:T(8,128)(2,1)S(1)}, bf16[4,128,128]{2,1,0:T(8,128)(2,1)S(1)}, u32[]{:S(2)}, u32[]{:S(2)}) collective-permute-start(bf16[4,128,128]{2,1,0:T(8,128)(2,1)S(1)} %collective-permute-done.7.refs_6_), channel_id=1, source_target_pairs={{0,1},{1,0},{2,3},{3,2},{4,5},{5,4},{6,7},{7,6},{8,9},{9,8},{10,11... | collective-permute-start | bytes 393224 | tf_op jit(solution)/shard_map/ppermute | solution.py:247
  20.8 11.0 %copy-start = (f32[85,512]{1,0:T(8,128)}, f32[85,512]{1,0:T(8,128)S(1)}, u32[]{:S(2)}) copy-start(f32[85,512]{1,0:T(8,128)S(1)} %collective-permute-done.inner_ref.refs_8_) | copy-start | bytes 522244
  21.9 9.9 %copy-start.1 = (f32[85,512]{1,0:T(8,128)}, f32[85,512]{1,0:T(8,128)S(1)}, u32[]{:S(2)}) copy-start(f32[85,512]{1,0:T(8,128)S(1)} %collective-permute-done.1.outer_ref.refs_9_) | copy-start | bytes 522244
  21.9 9.9 %copy-start.7 = (bf16[4,128,128]{2,1,0:T(8,128)(2,1)}, bf16[4,128,128]{2,1,0:T(8,128)(2,1)S(1)}, u32[]{:S(2)}) copy-start(bf16[4,128,128]{2,1,0:T(8,128)(2,1)S(1)} %collective-permute-done.4.refs_3_) | copy-start | bytes 393220
  21.9 9.9 %copy-start.8 = (bf16[4,128,128]{2,1,0:T(8,128)(2,1)}, bf16[4,128,128]{2,1,0:T(8,128)(2,1)S(1)}, u32[]{:S(2)}) copy-start(bf16[4,128,128]{2,1,0:T(8,128)(2,1)S(1)} %collective-permute-done.6.refs_5_) | copy-start | bytes 393220
  21.9 9.9 %copy-start.9 = (bf16[4,128,128]{2,1,0:T(8,128)(2,1)}, bf16[4,128,128]{2,1,0:T(8,128)(2,1)S(1)}, u32[]{:S(2)}) copy-start(bf16[4,128,128]{2,1,0:T(8,128)(2,1)S(1)} %collective-permute-done.8.refs_7_) | copy-start | bytes 393220
  36.0 25.1 %all-to-all-start.1 = ((bf16[16,64,640]{2,1,0:T(8,128)(2,1)}), bf16[16,64,640]{2,1,0:T(8,128)(2,1)S(1)}, u32[]{:S(2)}, u32[]{:S(2)}) async-start(bf16[16,64,640]{2,1,0:T(8,128)(2,1)} %shard_map.89), calls=%async_computation.1 | async-start | bytes 2621440 | tf_op jit(solution)/shard_map/all_to_all | solution.py:322

commit v5 on v4

--- a/solution.py
+++ b/solution.py
@@ -293,9 +293,8 @@
         scratch_shapes=[pltpu.VMEM((NP // lanes, NT * F * LAYERS, lanes), f32), dma((NP // lanes,))],
     )
     size = lax.axis_size(RADIAL)
-    joints = [(i, (i + 1) % size) for i in range(1, size, 2)]
-    inner = shift(inner, "core", 1)
-    outer = lax.ppermute(outer, RADIAL, joints + [(j, i) for i, j in joints])
+    inner, relayed = shift(inner, "core", 1), shift(outer, "core", 1)
+    outer = lax.ppermute(relayed, RADIAL, [(i, (i + 2 - 4 * (i % 2)) % size) for i in range(size)])
 
     weights, time_faces = call(
         weights_kernel,
@@ -304,13 +303,13 @@
         2 * ROWS * ROWS * SLOTS,
     )
 
-    inner, outer = in_hbm(inner, outer)
+    (outer,) = in_hbm(outer)
     products = call(
         maps_kernel,
         pltpu.HBM((PEERS, SLOTS // PEERS, WIDTH), bf16),
-        (in_vmem(arrived), *in_hbm(*pieces), inner, outer),
+        (in_vmem(arrived), *in_hbm(*pieces), outer),
         2 * SLOTS * F * 8 * FACE * FACE,
-        in_specs=[vmem] + [hbm] * 10,
+        in_specs=[vmem] + [hbm] * 9,
         out_specs=hbm,
         scratch_shapes=[
             pltpu.VMEM((4, 2, 4, FACE, FACE), bf16),

time: 65.3 us -> 64.7 us (level)
  waiting for transfers between devices: 26.5 us -> 22.2 us
  starting transfers between devices: 15.4 us -> 18.5 us
  local copies, waits for them, and re-layouts: 0.04 us -> 0.71 us
    all_to_all x1, waiting for transfers between devices: 9.85 us -> 3.79 us  [body(): lax.all_to_all(outgoing.reshape(PEERS, SLOTS // PEERS, WIDTH), SPREAD, 0,...]
    ppermute x1, starting transfers between devices: 0.58 us -> 3.88 us  [body(): lax.ppermute(relayed, RADIAL, [(i, (i + 2 - 4 * (i % 2)) % size) for i in...]
    ppermute x1, waiting for transfers between devices: 1.12 us -> 3.12 us  [body(): lax.ppermute(relayed, RADIAL, [(i, (i + 2 - 4 * (i % 2)) % size) for i in...]
    all_to_all x1, waiting for transfers between devices: 12.3 us -> 11.1 us  [body(): returned = lax.all_to_all(products, SPREAD, 0, 0, tiled=True)]
    ppermute x8 -> x9, waiting for transfers between devices: 3.25 us -> 4.15 us  [shift(): lax.ppermute(value, axis, [(i, (i + step) % size) for i in range(size)])]
    unnamed x20, local copies, waits for them, and re-layouts: 0.04 us -> 0.71 us
    ppermute x8 -> x9, starting transfers between devices: 3.93 us -> 3.82 us  [shift(): lax.ppermute(value, axis, [(i, (i + step) % size) for i in range(size)])]
  transfers between devices with their start and end apart: 11 -> 12, of which waited for: 5 -> 6; matrix products, arithmetic and copies ran while one was open for 0% -> 0% of each run, Pallas kernels for 17% -> 17%
where the time goes in v5:
time: 64.7 us; the launch traced here: 64.3 us
  waiting for transfers between devices  22.2 us (34%)
  Pallas kernels  22.1 us (34%)
  starting transfers between devices  18.5 us (29%)
  between operations  0.79 us (1%)
  local copies, waits for them, and re-layouts  0.71 us (1%)
    pallas_call x6, Pallas kernels, call(): pl.pallas_call(kernel, out_shape=outs, compiler_params=pltpu.CompilerPara...  22.1 us
    all_to_all x1, waiting for transfers between devices, body(): returned = lax.all_to_all(products, SPREAD, 0, 0, tiled=True)  11.1 us
    all_to_all x1, starting transfers between devices, body(): lax.all_to_all(outgoing.reshape(PEERS, SLOTS // PEERS, WIDTH), SPREAD, 0,...  7.06 us
    ppermute x9, waiting for transfers between devices, shift(): lax.ppermute(value, axis, [(i, (i + step) % size) for i in range(size)])  4.15 us
    ppermute x1, starting transfers between devices, body(): lax.ppermute(relayed, RADIAL, [(i, (i + 2 - 4 * (i % 2)) % size) for i in...  3.88 us
    ppermute x9, starting transfers between devices, shift(): lax.ppermute(value, axis, [(i, (i + step) % size) for i in range(size)])  3.82 us
    all_to_all x1, waiting for transfers between devices, body(): lax.all_to_all(outgoing.reshape(PEERS, SLOTS // PEERS, WIDTH), SPREAD, 0,...  3.79 us
    all_to_all x1, starting transfers between devices, body(): returned = lax.all_to_all(products, SPREAD, 0, 0, tiled=True)  3.71 us
  transfers between devices with their start and end apart: 12, of which 6 were waited for; matrix products, arithmetic and copies ran while one was open for 0% of the time, Pallas kernels for 17%

profile of v5, /device:TPU:96, one launch (start us, length us, event | category | flops | bytes accessed | tf_op | source)
XLA Modules:
  0.0 64.3 jit_solution(13180503618393378832)
XLA Ops:
  0.6 3.1 %shard_map.88 = bf16[1024,640]{1,0:T(8,128)(2,1)} custom-call(f32[17,5,16,128]{3,2,1,0:T(8,128)} %bitcast.24, s32[3,16,17]{2,1,0:T(8,128)} %bitcast.29), custom_call_target="tpu_custom_call" | custom-call | flops 713031680 | bytes 2010304 | tf_op jit(solution)/shard_map/pallas_call | solution.py:236
  3.7 7.1 %all-to-all-start = ((bf16[16,64,640]{2,1,0:T(8,128)(2,1)}), bf16[16,64,640]{2,1,0:T(8,128)(2,1)S(1)}, u32[]{:S(2)}, u32[]{:S(2)}) async-start(bf16[16,64,640]{2,1,0:T(8,128)(2,1)} %bitcast.23), calls=%async_computation | async-start | bytes 2621440 | tf_op jit(solution)/shard_map/all_to_all | solution.py:278
  10.8 0.0 copy-start.2
  10.8 2.1 %shard_map.86 = (f32[85,512]{1,0:T(8,128)S(1)}, f32[85,512]{1,0:T(8,128)S(1)}) custom-call(f32[680,512]{1,0:T(8,128)} %bitcast.19, f32[8,512]{1,0:T(8,128)} %bitcast.27), custom_call_target="tpu_custom_call" | custom-call | bytes 1757184 | tf_op jit(solution)/shard_map/pallas_call | solution.py:236
  12.9 0.1 collective-permute-start.1
  13.0 0.1 collective-permute-start.4
  13.1 2.0 %collective-permute-start.6 = (bf16[4,128,128]{2,1,0:T(8,128)(2,1)S(1)}, bf16[4,128,128]{2,1,0:T(8,128)(2,1)S(1)}, u32[]{:S(2)}, u32[]{:S(2)}) collective-permute-start(bf16[4,128,128]{2,1,0:T(8,128)(2,1)S(1)} %copy-done.2), channel_id=1, source_target_pairs={{0,6},{2,0},{4,2},{6,4},{1,7},{3,1},{5,3},{7,5},{8,14},{10,8},{12,... | collective-permute-start | bytes 393224 | tf_op jit(solution)/shard_map/ppermute | solution.py:247
  15.1 0.6 collective-permute-start.8
  15.7 0.0 collective-permute-done.1
  15.7 3.9 %collective-permute-start.2 = (f32[85,512]{1,0:T(8,128)S(1)}, f32[85,512]{1,0:T(8,128)S(1)}, u32[]{:S(2)}, u32[]{:S(2)}) collective-permute-start(f32[85,512]{1,0:T(8,128)S(1)} %collective-permute-done.1), channel_id=1, source_target_pairs={{0,2},{1,31},{2,4},{3,1},{4,6},{5,3},{6,8},{7,5},{8,10},{9,7},{10,... | collective-permute-start | bytes 522248 | tf_op jit(solution)/shard_map/ppermute | solution.py:297
  19.5 0.0 collective-permute-start.3
  19.5 0.0 collective-permute-done.4.refs_2_
  19.5 0.5 collective-permute-start.5
  20.1 3.1 %collective-permute-done.6.refs_4_ = bf16[4,128,128]{2,1,0:T(8,128)(2,1)S(1)} collective-permute-done((bf16[4,128,128]{2,1,0:T(8,128)(2,1)S(1)}, bf16[4,128,128]{2,1,0:T(8,128)(2,1)S(1)}, u32[]{:S(2)}, u32[]{:S(2)}) %collective-permute-start.6) | collective-permute-done | bytes 131104 | tf_op jit(solution)/shard_map/ppermute | solution.py:247
  23.2 0.0 collective-permute-start.7
  23.2 0.0 collective-permute-done.8.refs_6_
  23.2 0.5 collective-permute-start.9
  23.7 0.0 collective-permute-done.3.refs_1_
  23.7 0.0 collective-permute-done.5.refs_3_
  23.7 0.8 %collective-permute-done.7.refs_5_ = bf16[4,128,128]{2,1,0:T(8,128)(2,1)S(1)} collective-permute-done((bf16[4,128,128]{2,1,0:T(8,128)(2,1)S(1)}, bf16[4,128,128]{2,1,0:T(8,128)(2,1)S(1)}, u32[]{:S(2)}, u32[]{:S(2)}) %collective-permute-start.7) | collective-permute-done | bytes 131104 | tf_op jit(solution)/shard_map/ppermute | solution.py:247
  24.6 0.2 collective-permute-done.9.refs_7_
  24.7 3.1 %collective-permute-done.2.outer_ref.refs_8_ = f32[85,512]{1,0:T(8,128)S(1)} collective-permute-done((f32[85,512]{1,0:T(8,128)S(1)}, f32[85,512]{1,0:T(8,128)S(1)}, u32[]{:S(2)}, u32[]{:S(2)}) %collective-permute-start.2) | collective-permute-done | bytes 174112 | tf_op jit(solution)/shard_map/ppermute | solution.py:297
  27.9 3.8 %all-to-all-done.rows_ref = bf16[16,64,640]{2,1,0:T(8,128)(2,1)S(1)} async-done(((bf16[16,64,640]{2,1,0:T(8,128)(2,1)}), bf16[16,64,640]{2,1,0:T(8,128)(2,1)S(1)}, u32[]{:S(2)}, u32[]{:S(2)}) %all-to-all-start) | async-done | bytes 1310752 | tf_op jit(solution)/shard_map/all_to_all | solution.py:278
  31.7 4.2 %shard_map.89 = bf16[16,64,640]{2,1,0:T(8,128)(2,1)} custom-call(bf16[16,64,640]{2,1,0:T(8,128)(2,1)S(1)} %all-to-all-done.rows_ref, bf16[4,128,128]{2,1,0:T(8,128)(2,1)} %refs_0_.1, bf16[4,128,128]{2,1,0:T(8,128)(2,1)} %copy-done.6, bf16[4,128,128]{2,1,0:T(8,128)(2,1)} %copy-done.3, bf16[4,128,128]{2,1,0:T(8,128)(2,1)} %copy-done.7, ...), custom_call_target="tpu_custom_call" | custom-call | flops 1342177280 | bytes 3844096 | tf_op jit(solution)/shard_map/pallas_call | solution.py:236
  35.9 3.7 %all-to-all-start.1 = ((bf16[16,64,640]{2,1,0:T(8,128)(2,1)}), bf16[16,64,640]{2,1,0:T(8,128)(2,1)S(1)}, u32[]{:S(2)}, u32[]{:S(2)}) async-start(bf16[16,64,640]{2,1,0:T(8,128)(2,1)} %shard_map.89), calls=%async_computation.1 | async-start | bytes 2621440 | tf_op jit(solution)/shard_map/all_to_all | solution.py:321
  39.6 0.1 collective-permute-start
  39.7 3.9 %shard_map.90 = (bf16[2,272,1024]{2,1,0:T(8,128)(2,1)}, f32[17,5,16,128]{3,2,1,0:T(8,128)}) custom-call(f32[17,5,16,128]{3,2,1,0:T(8,128)} %bitcast.25, s32[3,16,17]{2,1,0:T(8,128)} %bitcast.30, f32[3,16,17]{2,1,0:T(8,128)} %bitcast.31), custom_call_target="tpu_custom_call" | custom-call | flops 151519232 | bytes 2513280 | tf_op jit(solution)/shard_map/pallas_call | solution.py:236
  43.6 0.0 collective-permute-done.inner_ref
  43.6 0.7 %copy-done.1 = f32[85,512]{1,0:T(8,128)} copy-done((f32[85,512]{1,0:T(8,128)}, f32[85,512]{1,0:T(8,128)S(1)}, u32[]{:S(2)}) %copy-start.1) | copy-done | bytes 174104
  44.2 5.2 %shard_map.87 = f32[17,5,8,512]{3,2,1,0:T(8,128)} custom-call(f32[17,5,8,512]{3,2,1,0:T(8,128)} %bitcast.20, bf16[17,5,5,8,512]{4,3,2,1,0:T(8,128)(2,1)} %bitcast.21, f32[8,512]{1,0:T(8,128)} %bitcast.28, f32[85,512]{1,0:T(8,128)} %copy-done.1, f32[85,512]{1,0:T(8,128)} %copy-done), custom_call_target="tpu_custom_call" | custom-call | flops 8355840 | bytes 6631424 | tf_op jit(solution)/shard_map/pallas_call | solution.py:236
  49.5 11.1 %all-to-all-done.1 = bf16[16,64,640]{2,1,0:T(8,128)(2,1)S(1)} async-done(((bf16[16,64,640]{2,1,0:T(8,128)(2,1)}), bf16[16,64,640]{2,1,0:T(8,128)(2,1)S(1)}, u32[]{:S(2)}, u32[]{:S(2)}) %all-to-all-start.1) | async-done | bytes 1310752 | tf_op jit(solution)/shard_map/all_to_all | solution.py:321
  60.6 3.7 %shard_map.91 = f32[17,5,16,128]{3,2,1,0:T(8,128)} custom-call(bf16[1024,640]{1,0:T(8,128)(2,1)S(1)} %bitcast.18, bf16[2,272,1024]{2,1,0:T(8,128)(2,1)} %get-tuple-element.8.weight_hbm, f32[17,5,16,128]{3,2,1,0:T(8,128)} %get-tuple-element.9.time_hbm), custom_call_target="tpu_custom_call" | custom-call | flops 713031680 | bytes 3817472 | tf_op jit(solution)/shard_map/pallas_call | solution.py:236
  (18 shorter events, 0.0 us)
Async XLA Ops:
  3.7 28.0 %all-to-all-start = ((bf16[16,64,640]{2,1,0:T(8,128)(2,1)}), bf16[16,64,640]{2,1,0:T(8,128)(2,1)S(1)}, u32[]{:S(2)}, u32[]{:S(2)}) async-start(bf16[16,64,640]{2,1,0:T(8,128)(2,1)} %bitcast.23), calls=%async_computation | async-start | bytes 2621440 | tf_op jit(solution)/shard_map/all_to_all | solution.py:278
  10.8 2.2 %copy-start.2 = (bf16[4,128,128]{2,1,0:T(8,128)(2,1)S(1)}, bf16[4,128,128]{2,1,0:T(8,128)(2,1)}, u32[]{:S(2)}) copy-start(bf16[4,128,128]{2,1,0:T(8,128)(2,1)} %refs_0_.1) | copy-start | bytes 393220
  12.9 2.8 %collective-permute-start.1 = (f32[85,512]{1,0:T(8,128)S(1)}, f32[85,512]{1,0:T(8,128)S(1)}, u32[]{:S(2)}, u32[]{:S(2)}) collective-permute-start(f32[85,512]{1,0:T(8,128)S(1)} %get-tuple-element.7), channel_id=1, source_target_pairs={{0,1},{1,0},{2,3},{3,2},{4,5},{5,4},{6,7},{7,6},{8,9},{9,8},{10,11... | collective-permute-start | bytes 522248 | tf_op jit(solution)/shard_map/ppermute | solution.py:247
  13.0 6.5 %collective-permute-start.4 = (bf16[4,128,128]{2,1,0:T(8,128)(2,1)S(1)}, bf16[4,128,128]{2,1,0:T(8,128)(2,1)S(1)}, u32[]{:S(2)}, u32[]{:S(2)}) collective-permute-start(bf16[4,128,128]{2,1,0:T(8,128)(2,1)S(1)} %copy-done.2), channel_id=1, source_target_pairs={{0,2},{2,4},{4,6},{6,0},{1,3},{3,5},{5,7},{7,1},{8,10},{10,12},{12... | collective-permute-start | bytes 393224 | tf_op jit(solution)/shard_map/ppermute | solution.py:247
  13.1 10.1 %collective-permute-start.6 = (bf16[4,128,128]{2,1,0:T(8,128)(2,1)S(1)}, bf16[4,128,128]{2,1,0:T(8,128)(2,1)S(1)}, u32[]{:S(2)}, u32[]{:S(2)}) collective-permute-start(bf16[4,128,128]{2,1,0:T(8,128)(2,1)S(1)} %copy-done.2), channel_id=1, source_target_pairs={{0,6},{2,0},{4,2},{6,4},{1,7},{3,1},{5,3},{7,5},{8,14},{10,8},{12,... | collective-permute-start | bytes 393224 | tf_op jit(solution)/shard_map/ppermute | solution.py:247
  15.1 8.1 %collective-permute-start.8 = (bf16[4,128,128]{2,1,0:T(8,128)(2,1)S(1)}, bf16[4,128,128]{2,1,0:T(8,128)(2,1)S(1)}, u32[]{:S(2)}, u32[]{:S(2)}) collective-permute-start(bf16[4,128,128]{2,1,0:T(8,128)(2,1)S(1)} %copy-done.2), channel_id=1, source_target_pairs={{0,4},{2,6},{4,0},{6,2},{1,5},{3,7},{5,1},{7,3},{8,12},{10,14},{12... | collective-permute-start | bytes 393224 | tf_op jit(solution)/shard_map/ppermute | solution.py:247
  15.7 12.2 %collective-permute-start.2 = (f32[85,512]{1,0:T(8,128)S(1)}, f32[85,512]{1,0:T(8,128)S(1)}, u32[]{:S(2)}, u32[]{:S(2)}) collective-permute-start(f32[85,512]{1,0:T(8,128)S(1)} %collective-permute-done.1), channel_id=1, source_target_pairs={{0,2},{1,31},{2,4},{3,1},{4,6},{5,3},{6,8},{7,5},{8,10},{9,7},{10,... | collective-permute-start | bytes 522248 | tf_op jit(solution)/shard_map/ppermute | solution.py:297
  19.5 4.2 %collective-permute-start.3 = (bf16[4,128,128]{2,1,0:T(8,128)(2,1)S(1)}, bf16[4,128,128]{2,1,0:T(8,128)(2,1)S(1)}, u32[]{:S(2)}, u32[]{:S(2)}) collective-permute-start(bf16[4,128,128]{2,1,0:T(8,128)(2,1)S(1)} %copy-done.2), channel_id=1, source_target_pairs={{0,1},{1,0},{2,3},{3,2},{4,5},{5,4},{6,7},{7,6},{8,9},{9,8},{10,11... | collective-permute-start | bytes 393224 | tf_op jit(solution)/shard_map/ppermute | solution.py:247
  19.5 12.1 %copy-start.3 = (bf16[4,128,128]{2,1,0:T(8,128)(2,1)}, bf16[4,128,128]{2,1,0:T(8,128)(2,1)S(1)}, u32[]{:S(2)}) copy-start(bf16[4,128,128]{2,1,0:T(8,128)(2,1)S(1)} %collective-permute-done.4.refs_2_) | copy-start | bytes 393220
  19.5 4.2 %collective-permute-start.5 = (bf16[4,128,128]{2,1,0:T(8,128)(2,1)S(1)}, bf16[4,128,128]{2,1,0:T(8,128)(2,1)S(1)}, u32[]{:S(2)}, u32[]{:S(2)}) collective-permute-start(bf16[4,128,128]{2,1,0:T(8,128)(2,1)S(1)} %collective-permute-done.4.refs_2_), channel_id=1, source_target_pairs={{0,1},{1,0},{2,3},{3,2},{4,5},{5,4},{6,7},{7,6},{8,9},{9,8},{10,11... | collective-permute-start | bytes 393224 | tf_op jit(solution)/shard_map/ppermute | solution.py:247
  23.2 8.5 %copy-start.4 = (bf16[4,128,128]{2,1,0:T(8,128)(2,1)}, bf16[4,128,128]{2,1,0:T(8,128)(2,1)S(1)}, u32[]{:S(2)}) copy-start(bf16[4,128,128]{2,1,0:T(8,128)(2,1)S(1)} %collective-permute-done.6.refs_4_) | copy-start | bytes 393220
  23.2 1.3 %collective-permute-start.7 = (bf16[4,128,128]{2,1,0:T(8,128)(2,1)S(1)}, bf16[4,128,128]{2,1,0:T(8,128)(2,1)S(1)}, u32[]{:S(2)}, u32[]{:S(2)}) collective-permute-start(bf16[4,128,128]{2,1,0:T(8,128)(2,1)S(1)} %collective-permute-done.6.refs_4_), channel_id=1, source_target_pairs={{0,1},{1,0},{2,3},{3,2},{4,5},{5,4},{6,7},{7,6},{8,9},{9,8},{10,11... | collective-permute-start | bytes 393224 | tf_op jit(solution)/shard_map/ppermute | solution.py:247
  23.2 8.4 %copy-start.5 = (bf16[4,128,128]{2,1,0:T(8,128)(2,1)}, bf16[4,128,128]{2,1,0:T(8,128)(2,1)S(1)}, u32[]{:S(2)}) copy-start(bf16[4,128,128]{2,1,0:T(8,128)(2,1)S(1)} %collective-permute-done.8.refs_6_) | copy-start | bytes 393220
  23.2 1.5 %collective-permute-start.9 = (bf16[4,128,128]{2,1,0:T(8,128)(2,1)S(1)}, bf16[4,128,128]{2,1,0:T(8,128)(2,1)S(1)}, u32[]{:S(2)}, u32[]{:S(2)}) collective-permute-start(bf16[4,128,128]{2,1,0:T(8,128)(2,1)S(1)} %collective-permute-done.8.refs_6_), channel_id=1, source_target_pairs={{0,1},{1,0},{2,3},{3,2},{4,5},{5,4},{6,7},{7,6},{8,9},{9,8},{10,11... | collective-permute-start | bytes 393224 | tf_op jit(solution)/shard_map/ppermute | solution.py:247
  23.7 7.9 %copy-start.6 = (bf16[4,128,128]{2,1,0:T(8,128)(2,1)}, bf16[4,128,128]{2,1,0:T(8,128)(2,1)S(1)}, u32[]{:S(2)}) copy-start(bf16[4,128,128]{2,1,0:T(8,128)(2,1)S(1)} %collective-permute-done.3.refs_1_) | copy-start | bytes 393220
  23.7 7.9 %copy-start.7 = (bf16[4,128,128]{2,1,0:T(8,128)(2,1)}, bf16[4,128,128]{2,1,0:T(8,128)(2,1)S(1)}, u32[]{:S(2)}) copy-start(bf16[4,128,128]{2,1,0:T(8,128)(2,1)S(1)} %collective-permute-done.5.refs_3_) | copy-start | bytes 393220
  24.5 7.1 %copy-start.8 = (bf16[4,128,128]{2,1,0:T(8,128)(2,1)}, bf16[4,128,128]{2,1,0:T(8,128)(2,1)S(1)}, u32[]{:S(2)}) copy-start(bf16[4,128,128]{2,1,0:T(8,128)(2,1)S(1)} %collective-permute-done.7.refs_5_) | copy-start | bytes 393220
  24.7 7.0 %copy-start.9 = (bf16[4,128,128]{2,1,0:T(8,128)(2,1)}, bf16[4,128,128]{2,1,0:T(8,128)(2,1)S(1)}, u32[]{:S(2)}) copy-start(bf16[4,128,128]{2,1,0:T(8,128)(2,1)S(1)} %collective-permute-done.9.refs_7_) | copy-start | bytes 393220
  27.9 3.8 %copy-start = (f32[85,512]{1,0:T(8,128)}, f32[85,512]{1,0:T(8,128)S(1)}, u32[]{:S(2)}) copy-start(f32[85,512]{1,0:T(8,128)S(1)} %collective-permute-done.2.outer_ref.refs_8_) | copy-start | bytes 522244
  35.9 24.7 %all-to-all-start.1 = ((bf16[16,64,640]{2,1,0:T(8,128)(2,1)}), bf16[16,64,640]{2,1,0:T(8,128)(2,1)S(1)}, u32[]{:S(2)}, u32[]{:S(2)}) async-start(bf16[16,64,640]{2,1,0:T(8,128)(2,1)} %shard_map.89), calls=%async_computation.1 | async-start | bytes 2621440 | tf_op jit(solution)/shard_map/all_to_all | solution.py:321
  39.6 4.0 %collective-permute-start = (f32[85,512]{1,0:T(8,128)S(1)}, f32[85,512]{1,0:T(8,128)S(1)}, u32[]{:S(2)}, u32[]{:S(2)}) collective-permute-start(f32[85,512]{1,0:T(8,128)S(1)} %get-tuple-element.6), channel_id=1, source_target_pairs={{0,1},{1,0},{2,3},{3,2},{4,5},{5,4},{6,7},{7,6},{8,9},{9,8},{10,11... | collective-permute-start | bytes 522248 | tf_op jit(solution)/shard_map/ppermute | solution.py:247
  43.6 0.7 %copy-start.1 = (f32[85,512]{1,0:T(8,128)}, f32[85,512]{1,0:T(8,128)S(1)}, u32[]{:S(2)}) copy-start(f32[85,512]{1,0:T(8,128)S(1)} %collective-permute-done.inner_ref) | copy-start | bytes 522244

commit v6 on v5

--- a/solution.py
+++ b/solution.py
@@ -27,7 +27,7 @@
 
 SPREAD = ("x", "y")
 STEPS = (0, 1, 3, 2)
-PARTS = 4
+PARTS = 2
 RADIAL = ("y", "z", "core")
 f32 = jnp.float32
 bf16 = jnp.bfloat16

time: 64.7 us -> 64.8 us (level)
  no operation moved by 1% of the time
where the time goes in v6:
time: 64.8 us; the launch traced here: 64.4 us
  Pallas kernels  22.2 us (34%)
  waiting for transfers between devices  22.2 us (34%)
  starting transfers between devices  18.5 us (29%)
  between operations  0.79 us (1%)
  local copies, waits for them, and re-layouts  0.71 us (1%)
    pallas_call x6, Pallas kernels, call(): pl.pallas_call(kernel, out_shape=outs, compiler_params=pltpu.CompilerPara...  22.2 us
    all_to_all x1, waiting for transfers between devices, body(): returned = lax.all_to_all(products, SPREAD, 0, 0, tiled=True)  11.1 us
    all_to_all x1, starting transfers between devices, body(): lax.all_to_all(outgoing.reshape(PEERS, SLOTS // PEERS, WIDTH), SPREAD, 0,...  7.05 us
    ppermute x9, waiting for transfers between devices, shift(): lax.ppermute(value, axis, [(i, (i + step) % size) for i in range(size)])  4.15 us
    ppermute x1, starting transfers between devices, body(): lax.ppermute(relayed, RADIAL, [(i, (i + 2 - 4 * (i % 2)) % size) for i in...  3.88 us
    ppermute x9, starting transfers between devices, shift(): lax.ppermute(value, axis, [(i, (i + step) % size) for i in range(size)])  3.82 us
    all_to_all x1, waiting for transfers between devices, body(): lax.all_to_all(outgoing.reshape(PEERS, SLOTS // PEERS, WIDTH), SPREAD, 0,...  3.79 us
    all_to_all x1, starting transfers between devices, body(): returned = lax.all_to_all(products, SPREAD, 0, 0, tiled=True)  3.71 us
  transfers between devices with their start and end apart: 12, of which 6 were waited for; matrix products, arithmetic and copies ran while one was open for 0% of the time, Pallas kernels for 17%

profile of v6, /device:TPU:96, one launch (start us, length us, event | category | flops | bytes accessed | tf_op | source)
XLA Modules:
  0.0 64.4 jit_solution(6411235155493663046)
XLA Ops:
  0.6 3.2 %shard_map.88 = bf16[1024,640]{1,0:T(8,128)(2,1)} custom-call(f32[17,5,16,128]{3,2,1,0:T(8,128)} %bitcast.24, s32[3,16,17]{2,1,0:T(8,128)} %bitcast.29), custom_call_target="tpu_custom_call" | custom-call | flops 713031680 | bytes 2010304 | tf_op jit(solution)/shard_map/pallas_call | solution.py:236
  3.8 7.1 %all-to-all-start = ((bf16[16,64,640]{2,1,0:T(8,128)(2,1)}), bf16[16,64,640]{2,1,0:T(8,128)(2,1)S(1)}, u32[]{:S(2)}, u32[]{:S(2)}) async-start(bf16[16,64,640]{2,1,0:T(8,128)(2,1)} %bitcast.23), calls=%async_computation | async-start | bytes 2621440 | tf_op jit(solution)/shard_map/all_to_all | solution.py:278
  10.9 0.0 copy-start.2
  10.9 2.1 %shard_map.86 = (f32[85,512]{1,0:T(8,128)S(1)}, f32[85,512]{1,0:T(8,128)S(1)}) custom-call(f32[680,512]{1,0:T(8,128)} %bitcast.19, f32[8,512]{1,0:T(8,128)} %bitcast.27), custom_call_target="tpu_custom_call" | custom-call | bytes 1757184 | tf_op jit(solution)/shard_map/pallas_call | solution.py:236
  13.0 0.1 collective-permute-start.1
  13.1 0.1 collective-permute-start.4
  13.2 2.0 %collective-permute-start.6 = (bf16[4,128,128]{2,1,0:T(8,128)(2,1)S(1)}, bf16[4,128,128]{2,1,0:T(8,128)(2,1)S(1)}, u32[]{:S(2)}, u32[]{:S(2)}) collective-permute-start(bf16[4,128,128]{2,1,0:T(8,128)(2,1)S(1)} %copy-done.2), channel_id=1, source_target_pairs={{0,6},{2,0},{4,2},{6,4},{1,7},{3,1},{5,3},{7,5},{8,14},{10,8},{12,... | collective-permute-start | bytes 393224 | tf_op jit(solution)/shard_map/ppermute | solution.py:247
  15.2 0.6 collective-permute-start.8
  15.7 0.0 collective-permute-done.1
  15.7 3.9 %collective-permute-start.2 = (f32[85,512]{1,0:T(8,128)S(1)}, f32[85,512]{1,0:T(8,128)S(1)}, u32[]{:S(2)}, u32[]{:S(2)}) collective-permute-start(f32[85,512]{1,0:T(8,128)S(1)} %collective-permute-done.1), channel_id=1, source_target_pairs={{0,2},{1,31},{2,4},{3,1},{4,6},{5,3},{6,8},{7,5},{8,10},{9,7},{10,... | collective-permute-start | bytes 522248 | tf_op jit(solution)/shard_map/ppermute | solution.py:297
  19.6 0.0 collective-permute-start.3
  19.6 0.0 collective-permute-done.4.refs_2_
  19.6 0.5 collective-permute-start.5
  20.1 3.1 %collective-permute-done.6.refs_4_ = bf16[4,128,128]{2,1,0:T(8,128)(2,1)S(1)} collective-permute-done((bf16[4,128,128]{2,1,0:T(8,128)(2,1)S(1)}, bf16[4,128,128]{2,1,0:T(8,128)(2,1)S(1)}, u32[]{:S(2)}, u32[]{:S(2)}) %collective-permute-start.6) | collective-permute-done | bytes 131104 | tf_op jit(solution)/shard_map/ppermute | solution.py:247
  23.3 0.0 collective-permute-start.7
  23.3 0.0 collective-permute-done.8.refs_6_
  23.3 0.5 collective-permute-start.9
  23.8 0.0 collective-permute-done.3.refs_1_
  23.8 0.0 collective-permute-done.5.refs_3_
  23.8 0.8 %collective-permute-done.7.refs_5_ = bf16[4,128,128]{2,1,0:T(8,128)(2,1)S(1)} collective-permute-done((bf16[4,128,128]{2,1,0:T(8,128)(2,1)S(1)}, bf16[4,128,128]{2,1,0:T(8,128)(2,1)S(1)}, u32[]{:S(2)}, u32[]{:S(2)}) %collective-permute-start.7) | collective-permute-done | bytes 131104 | tf_op jit(solution)/shard_map/ppermute | solution.py:247
  24.6 0.2 collective-permute-done.9.refs_7_
  24.8 3.1 %collective-permute-done.2.outer_ref.refs_8_ = f32[85,512]{1,0:T(8,128)S(1)} collective-permute-done((f32[85,512]{1,0:T(8,128)S(1)}, f32[85,512]{1,0:T(8,128)S(1)}, u32[]{:S(2)}, u32[]{:S(2)}) %collective-permute-start.2) | collective-permute-done | bytes 174112 | tf_op jit(solution)/shard_map/ppermute | solution.py:297
  28.0 3.8 %all-to-all-done.rows_ref = bf16[16,64,640]{2,1,0:T(8,128)(2,1)S(1)} async-done(((bf16[16,64,640]{2,1,0:T(8,128)(2,1)}), bf16[16,64,640]{2,1,0:T(8,128)(2,1)S(1)}, u32[]{:S(2)}, u32[]{:S(2)}) %all-to-all-start) | async-done | bytes 1310752 | tf_op jit(solution)/shard_map/all_to_all | solution.py:278
  31.8 4.1 %shard_map.89 = bf16[16,64,640]{2,1,0:T(8,128)(2,1)} custom-call(bf16[16,64,640]{2,1,0:T(8,128)(2,1)S(1)} %all-to-all-done.rows_ref, bf16[4,128,128]{2,1,0:T(8,128)(2,1)} %refs_0_.1, bf16[4,128,128]{2,1,0:T(8,128)(2,1)} %copy-done.6, bf16[4,128,128]{2,1,0:T(8,128)(2,1)} %copy-done.3, bf16[4,128,128]{2,1,0:T(8,128)(2,1)} %copy-done.7, ...), custom_call_target="tpu_custom_call" | custom-call | flops 1342177280 | bytes 3844096 | tf_op jit(solution)/shard_map/pallas_call | solution.py:236
  36.0 3.7 %all-to-all-start.1 = ((bf16[16,64,640]{2,1,0:T(8,128)(2,1)}), bf16[16,64,640]{2,1,0:T(8,128)(2,1)S(1)}, u32[]{:S(2)}, u32[]{:S(2)}) async-start(bf16[16,64,640]{2,1,0:T(8,128)(2,1)} %shard_map.89), calls=%async_computation.1 | async-start | bytes 2621440 | tf_op jit(solution)/shard_map/all_to_all | solution.py:321
  39.7 0.1 collective-permute-start
  39.8 3.9 %shard_map.90 = (bf16[2,272,1024]{2,1,0:T(8,128)(2,1)}, f32[17,5,16,128]{3,2,1,0:T(8,128)}) custom-call(f32[17,5,16,128]{3,2,1,0:T(8,128)} %bitcast.25, s32[3,16,17]{2,1,0:T(8,128)} %bitcast.30, f32[3,16,17]{2,1,0:T(8,128)} %bitcast.31), custom_call_target="tpu_custom_call" | custom-call | flops 151519232 | bytes 2513280 | tf_op jit(solution)/shard_map/pallas_call | solution.py:236
  43.7 0.0 collective-permute-done.inner_ref
  43.7 0.7 %copy-done.1 = f32[85,512]{1,0:T(8,128)} copy-done((f32[85,512]{1,0:T(8,128)}, f32[85,512]{1,0:T(8,128)S(1)}, u32[]{:S(2)}) %copy-start.1) | copy-done | bytes 174104
  44.3 5.2 %shard_map.87 = f32[17,5,8,512]{3,2,1,0:T(8,128)} custom-call(f32[17,5,8,512]{3,2,1,0:T(8,128)} %bitcast.20, bf16[17,5,5,8,512]{4,3,2,1,0:T(8,128)(2,1)} %bitcast.21, f32[8,512]{1,0:T(8,128)} %bitcast.28, f32[85,512]{1,0:T(8,128)} %copy-done.1, f32[85,512]{1,0:T(8,128)} %copy-done), custom_call_target="tpu_custom_call" | custom-call | flops 8355840 | bytes 6631424 | tf_op jit(solution)/shard_map/pallas_call | solution.py:236
  49.6 11.1 %all-to-all-done.1 = bf16[16,64,640]{2,1,0:T(8,128)(2,1)S(1)} async-done(((bf16[16,64,640]{2,1,0:T(8,128)(2,1)}), bf16[16,64,640]{2,1,0:T(8,128)(2,1)S(1)}, u32[]{:S(2)}, u32[]{:S(2)}) %all-to-all-start.1) | async-done | bytes 1310752 | tf_op jit(solution)/shard_map/all_to_all | solution.py:321
  60.7 3.7 %shard_map.91 = f32[17,5,16,128]{3,2,1,0:T(8,128)} custom-call(bf16[1024,640]{1,0:T(8,128)(2,1)S(1)} %bitcast.18, bf16[2,272,1024]{2,1,0:T(8,128)(2,1)} %get-tuple-element.8.weight_hbm, f32[17,5,16,128]{3,2,1,0:T(8,128)} %get-tuple-element.9.time_hbm), custom_call_target="tpu_custom_call" | custom-call | flops 713031680 | bytes 3817472 | tf_op jit(solution)/shard_map/pallas_call | solution.py:236
  (18 shorter events, 0.0 us)
Async XLA Ops:
  3.8 27.9 %all-to-all-start = ((bf16[16,64,640]{2,1,0:T(8,128)(2,1)}), bf16[16,64,640]{2,1,0:T(8,128)(2,1)S(1)}, u32[]{:S(2)}, u32[]{:S(2)}) async-start(bf16[16,64,640]{2,1,0:T(8,128)(2,1)} %bitcast.23), calls=%async_computation | async-start | bytes 2621440 | tf_op jit(solution)/shard_map/all_to_all | solution.py:278
  10.9 2.2 %copy-start.2 = (bf16[4,128,128]{2,1,0:T(8,128)(2,1)S(1)}, bf16[4,128,128]{2,1,0:T(8,128)(2,1)}, u32[]{:S(2)}) copy-start(bf16[4,128,128]{2,1,0:T(8,128)(2,1)} %refs_0_.1) | copy-start | bytes 393220
  13.0 2.8 %collective-permute-start.1 = (f32[85,512]{1,0:T(8,128)S(1)}, f32[85,512]{1,0:T(8,128)S(1)}, u32[]{:S(2)}, u32[]{:S(2)}) collective-permute-start(f32[85,512]{1,0:T(8,128)S(1)} %get-tuple-element.7), channel_id=1, source_target_pairs={{0,1},{1,0},{2,3},{3,2},{4,5},{5,4},{6,7},{7,6},{8,9},{9,8},{10,11... | collective-permute-start | bytes 522248 | tf_op jit(solution)/shard_map/ppermute | solution.py:247
  13.1 6.5 %collective-permute-start.4 = (bf16[4,128,128]{2,1,0:T(8,128)(2,1)S(1)}, bf16[4,128,128]{2,1,0:T(8,128)(2,1)S(1)}, u32[]{:S(2)}, u32[]{:S(2)}) collective-permute-start(bf16[4,128,128]{2,1,0:T(8,128)(2,1)S(1)} %copy-done.2), channel_id=1, source_target_pairs={{0,2},{2,4},{4,6},{6,0},{1,3},{3,5},{5,7},{7,1},{8,10},{10,12},{12... | collective-permute-start | bytes 393224 | tf_op jit(solution)/shard_map/ppermute | solution.py:247
  13.2 10.1 %collective-permute-start.6 = (bf16[4,128,128]{2,1,0:T(8,128)(2,1)S(1)}, bf16[4,128,128]{2,1,0:T(8,128)(2,1)S(1)}, u32[]{:S(2)}, u32[]{:S(2)}) collective-permute-start(bf16[4,128,128]{2,1,0:T(8,128)(2,1)S(1)} %copy-done.2), channel_id=1, source_target_pairs={{0,6},{2,0},{4,2},{6,4},{1,7},{3,1},{5,3},{7,5},{8,14},{10,8},{12,... | collective-permute-start | bytes 393224 | tf_op jit(solution)/shard_map/ppermute | solution.py:247
  15.2 8.1 %collective-permute-start.8 = (bf16[4,128,128]{2,1,0:T(8,128)(2,1)S(1)}, bf16[4,128,128]{2,1,0:T(8,128)(2,1)S(1)}, u32[]{:S(2)}, u32[]{:S(2)}) collective-permute-start(bf16[4,128,128]{2,1,0:T(8,128)(2,1)S(1)} %copy-done.2), channel_id=1, source_target_pairs={{0,4},{2,6},{4,0},{6,2},{1,5},{3,7},{5,1},{7,3},{8,12},{10,14},{12... | collective-permute-start | bytes 393224 | tf_op jit(solution)/shard_map/ppermute | solution.py:247
  15.7 12.2 %collective-permute-start.2 = (f32[85,512]{1,0:T(8,128)S(1)}, f32[85,512]{1,0:T(8,128)S(1)}, u32[]{:S(2)}, u32[]{:S(2)}) collective-permute-start(f32[85,512]{1,0:T(8,128)S(1)} %collective-permute-done.1), channel_id=1, source_target_pairs={{0,2},{1,31},{2,4},{3,1},{4,6},{5,3},{6,8},{7,5},{8,10},{9,7},{10,... | collective-permute-start | bytes 522248 | tf_op jit(solution)/shard_map/ppermute | solution.py:297
  19.6 4.2 %collective-permute-start.3 = (bf16[4,128,128]{2,1,0:T(8,128)(2,1)S(1)}, bf16[4,128,128]{2,1,0:T(8,128)(2,1)S(1)}, u32[]{:S(2)}, u32[]{:S(2)}) collective-permute-start(bf16[4,128,128]{2,1,0:T(8,128)(2,1)S(1)} %copy-done.2), channel_id=1, source_target_pairs={{0,1},{1,0},{2,3},{3,2},{4,5},{5,4},{6,7},{7,6},{8,9},{9,8},{10,11... | collective-permute-start | bytes 393224 | tf_op jit(solution)/shard_map/ppermute | solution.py:247
  19.6 12.1 %copy-start.3 = (bf16[4,128,128]{2,1,0:T(8,128)(2,1)}, bf16[4,128,128]{2,1,0:T(8,128)(2,1)S(1)}, u32[]{:S(2)}) copy-start(bf16[4,128,128]{2,1,0:T(8,128)(2,1)S(1)} %collective-permute-done.4.refs_2_) | copy-start | bytes 393220
  19.6 4.2 %collective-permute-start.5 = (bf16[4,128,128]{2,1,0:T(8,128)(2,1)S(1)}, bf16[4,128,128]{2,1,0:T(8,128)(2,1)S(1)}, u32[]{:S(2)}, u32[]{:S(2)}) collective-permute-start(bf16[4,128,128]{2,1,0:T(8,128)(2,1)S(1)} %collective-permute-done.4.refs_2_), channel_id=1, source_target_pairs={{0,1},{1,0},{2,3},{3,2},{4,5},{5,4},{6,7},{7,6},{8,9},{9,8},{10,11... | collective-permute-start | bytes 393224 | tf_op jit(solution)/shard_map/ppermute | solution.py:247
  23.3 8.5 %copy-start.4 = (bf16[4,128,128]{2,1,0:T(8,128)(2,1)}, bf16[4,128,128]{2,1,0:T(8,128)(2,1)S(1)}, u32[]{:S(2)}) copy-start(bf16[4,128,128]{2,1,0:T(8,128)(2,1)S(1)} %collective-permute-done.6.refs_4_) | copy-start | bytes 393220
  23.3 1.3 %collective-permute-start.7 = (bf16[4,128,128]{2,1,0:T(8,128)(2,1)S(1)}, bf16[4,128,128]{2,1,0:T(8,128)(2,1)S(1)}, u32[]{:S(2)}, u32[]{:S(2)}) collective-permute-start(bf16[4,128,128]{2,1,0:T(8,128)(2,1)S(1)} %collective-permute-done.6.refs_4_), channel_id=1, source_target_pairs={{0,1},{1,0},{2,3},{3,2},{4,5},{5,4},{6,7},{7,6},{8,9},{9,8},{10,11... | collective-permute-start | bytes 393224 | tf_op jit(solution)/shard_map/ppermute | solution.py:247
  23.3 8.4 %copy-start.5 = (bf16[4,128,128]{2,1,0:T(8,128)(2,1)}, bf16[4,128,128]{2,1,0:T(8,128)(2,1)S(1)}, u32[]{:S(2)}) copy-start(bf16[4,128,128]{2,1,0:T(8,128)(2,1)S(1)} %collective-permute-done.8.refs_6_) | copy-start | bytes 393220
  23.3 1.5 %collective-permute-start.9 = (bf16[4,128,128]{2,1,0:T(8,128)(2,1)S(1)}, bf16[4,128,128]{2,1,0:T(8,128)(2,1)S(1)}, u32[]{:S(2)}, u32[]{:S(2)}) collective-permute-start(bf16[4,128,128]{2,1,0:T(8,128)(2,1)S(1)} %collective-permute-done.8.refs_6_), channel_id=1, source_target_pairs={{0,1},{1,0},{2,3},{3,2},{4,5},{5,4},{6,7},{7,6},{8,9},{9,8},{10,11... | collective-permute-start | bytes 393224 | tf_op jit(solution)/shard_map/ppermute | solution.py:247
  23.8 7.9 %copy-start.6 = (bf16[4,128,128]{2,1,0:T(8,128)(2,1)}, bf16[4,128,128]{2,1,0:T(8,128)(2,1)S(1)}, u32[]{:S(2)}) copy-start(bf16[4,128,128]{2,1,0:T(8,128)(2,1)S(1)} %collective-permute-done.3.refs_1_) | copy-start | bytes 393220
  23.8 7.9 %copy-start.7 = (bf16[4,128,128]{2,1,0:T(8,128)(2,1)}, bf16[4,128,128]{2,1,0:T(8,128)(2,1)S(1)}, u32[]{:S(2)}) copy-start(bf16[4,128,128]{2,1,0:T(8,128)(2,1)S(1)} %collective-permute-done.5.refs_3_) | copy-start | bytes 393220
  24.6 7.1 %copy-start.8 = (bf16[4,128,128]{2,1,0:T(8,128)(2,1)}, bf16[4,128,128]{2,1,0:T(8,128)(2,1)S(1)}, u32[]{:S(2)}) copy-start(bf16[4,128,128]{2,1,0:T(8,128)(2,1)S(1)} %collective-permute-done.7.refs_5_) | copy-start | bytes 393220
  24.8 7.0 %copy-start.9 = (bf16[4,128,128]{2,1,0:T(8,128)(2,1)}, bf16[4,128,128]{2,1,0:T(8,128)(2,1)S(1)}, u32[]{:S(2)}) copy-start(bf16[4,128,128]{2,1,0:T(8,128)(2,1)S(1)} %collective-permute-done.9.refs_7_) | copy-start | bytes 393220
  27.9 3.8 %copy-start = (f32[85,512]{1,0:T(8,128)}, f32[85,512]{1,0:T(8,128)S(1)}, u32[]{:S(2)}) copy-start(f32[85,512]{1,0:T(8,128)S(1)} %collective-permute-done.2.outer_ref.refs_8_) | copy-start | bytes 522244
  36.0 24.7 %all-to-all-start.1 = ((bf16[16,64,640]{2,1,0:T(8,128)(2,1)}), bf16[16,64,640]{2,1,0:T(8,128)(2,1)S(1)}, u32[]{:S(2)}, u32[]{:S(2)}) async-start(bf16[16,64,640]{2,1,0:T(8,128)(2,1)} %shard_map.89), calls=%async_computation.1 | async-start | bytes 2621440 | tf_op jit(solution)/shard_map/all_to_all | solution.py:321
  39.7 4.0 %collective-permute-start = (f32[85,512]{1,0:T(8,128)S(1)}, f32[85,512]{1,0:T(8,128)S(1)}, u32[]{:S(2)}, u32[]{:S(2)}) collective-permute-start(f32[85,512]{1,0:T(8,128)S(1)} %get-tuple-element.6), channel_id=1, source_target_pairs={{0,1},{1,0},{2,3},{3,2},{4,5},{5,4},{6,7},{7,6},{8,9},{9,8},{10,11... | collective-permute-start | bytes 522248 | tf_op jit(solution)/shard_map/ppermute | solution.py:247
  43.7 0.7 %copy-start.1 = (f32[85,512]{1,0:T(8,128)}, f32[85,512]{1,0:T(8,128)S(1)}, u32[]{:S(2)}) copy-start(f32[85,512]{1,0:T(8,128)S(1)} %collective-permute-done.inner_ref) | copy-start | bytes 522244
